TPU v7x, 32 devices: a whole 2x2x4 slice. The times are simulated.
32 devices in a mesh: dp: 8 (over z, x), seq: 4 (over y, core).
Axes of the slice: x: 2, y: 2, z: 4, core: 2. Of those that a mesh axis runs over, the one named last changes fastest.
Arguments:
- patches: bfloat16 [48, 576, 768], P('dp', 'seq'), may hold values from -6 to 6
- targets: bfloat16 [48, 576, 768], P('dp', 'seq'), may hold values from -6 to 6
- mask_order: int32 [48, 576], P('dp', 'seq'), may hold values from 0 to 575, each once within a row
- mask_count: int32 [48], P('dp'), may hold values from 230 to 460
- attend_gain: bfloat16 [768], replicated, may hold values from 0.5 to 1.5
- attend_shift: bfloat16 [768], replicated, may hold values from -1 to 1
- joint_weight: bfloat16 [768, 2304], replicated, may hold values from -0.21875 to 0.21875
- query_bias: bfloat16 [768], replicated, may hold values from -1.5 to 1.5
- value_bias: bfloat16 [768], replicated, may hold values from -1.5 to 1.5
- output_weight: bfloat16 [768, 768], replicated, may hold values from -2 to 2
- output_bias: bfloat16 [768], replicated, may hold values from -1 to 1
- feed_gain: bfloat16 [768], replicated, may hold values from 0.5 to 1.5
- feed_shift: bfloat16 [768], replicated, may hold values from -1 to 1
- expand_weight: bfloat16 [768, 3072], replicated, may hold values from -0.21875 to 0.21875
- expand_bias: bfloat16 [3072], replicated, may hold values from -1.5 to 1.5
- reduce_weight: bfloat16 [3072, 768], replicated, may hold values from -0.15625 to 0.15625
- reduce_bias: bfloat16 [768], replicated, may hold values from -1 to 1
- pixel_weight: bfloat16 [768, 768], replicated, may hold values from -0.21875 to 0.21875
- pixel_bias: bfloat16 [768], replicated, may hold values from -1.5 to 1.5
- mask_token: bfloat16 [768], replicated, may hold values from -4 to 4
Outputs:
- loss_value: float32 [], replicated
- attend_gain_grad: float32 [768], P('dp')
- attend_shift_grad: float32 [768], P('dp')
- joint_weight_grad: float32 [768, 2304], P('dp')
- query_bias_grad: float32 [768], P('dp')
- value_bias_grad: float32 [768], P('dp')
- output_weight_grad: float32 [768, 768], P('dp')
- output_bias_grad: float32 [768], P('dp')
- feed_gain_grad: float32 [768], P('dp')
- feed_shift_grad: float32 [768], P('dp')
- expand_weight_grad: float32 [768, 3072], P('dp')
- expand_bias_grad: float32 [3072], P('dp')
- reduce_weight_grad: float32 [3072, 768], P('dp')
- reduce_bias_grad: float32 [768], P('dp')
- pixel_weight_grad: float32 [768, 768], P('dp')
- pixel_bias_grad: float32 [768], P('dp')
- mask_token_grad: float32 [768], P('dp')
- patch_grad: float32 [48, 576, 768], P('dp', 'seq')
Inputs may be any that keep to these rules, and one draw needn't show every extreme that they name: Each image's row holds every number below 576 once; patch p of image i is masked when mask_order[i, p] < mask_count[i].
All inputs are finite; a program needn't handle non-finite values.
Results may differ from a plain program's by a relative error of at most 0.011.
Values may be sent and summed in bfloat16 or wider, within the bound.
A program may use at most 192 MiB of HBM per device.

v0:
```python
from functools import partial

import jax
import jax.numpy as jnp
from jax import lax
from jax.sharding import PartitionSpec as P

HEADS = 12
HEAD_DIM = 64
PIXELS = 768


def normalize(inputs):
    centre = inputs - jnp.mean(inputs, axis=-1, keepdims=True)
    scaling = lax.rsqrt(jnp.mean(centre * centre, axis=-1, keepdims=True) + 1e-06)
    return (centre * scaling, scaling)


def normalize_back(upstream, normed, scaling, gain):
    scaled = upstream * gain
    return scaling * (
        scaled
        - jnp.mean(scaled, axis=-1, keepdims=True)
        - normed * jnp.mean(scaled * normed, axis=-1, keepdims=True)
    )


def outer_sum(left, right):
    return jnp.einsum("ra,rb->ab", left, right, preferred_element_type=jnp.float32)


def back_product(left, right):
    return jnp.einsum("rb,ab->ra", left, right, preferred_element_type=jnp.float32)


def column_sums(values):
    return jnp.sum(values.astype(jnp.float32), axis=0)


def on_device(
    patches,
    targets,
    mask_order,
    mask_count,
    attend_gain,
    attend_shift,
    joint_weight,
    query_bias,
    value_bias,
    output_weight,
    output_bias,
    feed_gain,
    feed_shift,
    expand_weight,
    expand_bias,
    reduce_weight,
    reduce_bias,
    pixel_weight,
    pixel_bias,
    mask_token,
):
    images, quarter, features = patches.shape
    seq_count = lax.axis_size("seq")
    row_count = images * quarter
    full_len = quarter * seq_count
    local_heads = HEADS // seq_count
    head_block = local_heads * HEAD_DIM
    score_scale = HEAD_DIM ** (-0.5)
    masked = (mask_order < mask_count[:, None]).reshape(row_count)
    mask_float = masked.astype(jnp.float32)
    embedded = jnp.where(
        masked[:, None],
        mask_token.astype(jnp.float32)[None, :],
        patches.reshape(row_count, features).astype(jnp.float32),
    )
    normed_one, scaling_one = normalize(embedded)
    gain_one = attend_gain.astype(jnp.float32)
    input_one = (normed_one * gain_one + attend_shift.astype(jnp.float32)).astype(jnp.bfloat16)
    joint_bias = jnp.concatenate(
        [
            query_bias.astype(jnp.float32),
            jnp.zeros((features,), jnp.float32),
            value_bias.astype(jnp.float32),
        ]
    )
    joint = (
        jnp.dot(input_one, joint_weight, preferred_element_type=jnp.float32) + joint_bias
    ).astype(jnp.bfloat16)
    joint = joint.reshape(images, quarter, 3, seq_count, head_block)
    by_heads = lax.all_to_all(joint, "seq", split_axis=3, concat_axis=1, tiled=True)
    by_heads = by_heads.reshape(images, full_len, 3, local_heads, HEAD_DIM)

    def attend(single):
        queries, keys_in, values_in = (single[:, 0], single[:, 1], single[:, 2])
        scores = (
            jnp.einsum("qhd,khd->hqk", queries, keys_in, preferred_element_type=jnp.float32)
            * score_scale
        )
        row_max = jnp.max(scores, axis=-1, keepdims=True)
        exponent = jnp.exp(scores - row_max)
        row_total = jnp.sum(exponent, axis=-1, keepdims=True)
        probs_low = (exponent / row_total).astype(jnp.bfloat16)
        mixed = jnp.einsum("hqk,khd->qhd", probs_low, values_in, preferred_element_type=jnp.float32)
        return (mixed.astype(jnp.bfloat16), (row_max + jnp.log(row_total))[..., 0])

    mixed_heads, log_total = lax.map(attend, by_heads)
    attn_rows = lax.all_to_all(
        mixed_heads.reshape(images, full_len, 1, head_block),
        "seq",
        split_axis=1,
        concat_axis=2,
        tiled=True,
    )
    attn_rows = attn_rows.reshape(row_count, features)
    after_attn = (
        embedded
        + jnp.dot(attn_rows, output_weight, preferred_element_type=jnp.float32)
        + output_bias.astype(jnp.float32)
    )
    normed_two, scaling_two = normalize(after_attn)
    gain_two = feed_gain.astype(jnp.float32)
    input_two = (normed_two * gain_two + feed_shift.astype(jnp.float32)).astype(jnp.bfloat16)
    expanded = jnp.dot(
        input_two, expand_weight, preferred_element_type=jnp.float32
    ) + expand_bias.astype(jnp.float32)
    activated, gelu_pull = jax.vjp(partial(jax.nn.gelu, approximate=False), expanded)
    activated = activated.astype(jnp.bfloat16)
    after_mlp = (
        after_attn
        + jnp.dot(activated, reduce_weight, preferred_element_type=jnp.float32)
        + reduce_bias.astype(jnp.float32)
    )
    after_low = after_mlp.astype(jnp.bfloat16)
    predicted = jnp.dot(
        after_low, pixel_weight, preferred_element_type=jnp.float32
    ) + pixel_bias.astype(jnp.float32)
    errors = predicted - targets.reshape(row_count, targets.shape[2]).astype(jnp.float32)
    smooth_root = jnp.sqrt(errors * errors + 1.0)
    channel_sums = jnp.sum((smooth_root - 1.0) * mask_float[:, None], axis=0)
    channel_total, count_sum = lax.psum((channel_sums, jnp.sum(mask_float)), ("dp", "seq"))
    inverse = 1.0 / (count_sum * PIXELS)
    loss_value = jnp.sum(channel_total) * inverse
    grad_pred = (mask_float[:, None] * errors / smooth_root * inverse).astype(jnp.bfloat16)
    pixel_weight_grad = outer_sum(after_low, grad_pred)
    pixel_bias_grad = column_sums(grad_pred)
    grad_mlp = back_product(grad_pred, pixel_weight)
    grad_branch = grad_mlp.astype(jnp.bfloat16)
    reduce_weight_grad = outer_sum(activated, grad_branch)
    reduce_bias_grad = column_sums(grad_branch)
    grad_expand = gelu_pull(back_product(grad_branch, reduce_weight))[0].astype(jnp.bfloat16)
    expand_weight_grad = outer_sum(input_two, grad_expand)
    expand_bias_grad = column_sums(grad_expand)
    grad_in_two = back_product(grad_expand, expand_weight)
    feed_gain_grad = jnp.sum(grad_in_two * normed_two, axis=0)
    feed_shift_grad = jnp.sum(grad_in_two, axis=0)
    grad_attn = grad_mlp + normalize_back(grad_in_two, normed_two, scaling_two, gain_two)
    grad_out = grad_attn.astype(jnp.bfloat16)
    output_weight_grad = outer_sum(attn_rows, grad_out)
    output_bias_grad = column_sums(grad_out)
    grad_mixed = back_product(grad_out, output_weight).astype(jnp.bfloat16)
    grad_heads = lax.all_to_all(
        grad_mixed.reshape(images, quarter, seq_count, head_block),
        "seq",
        split_axis=2,
        concat_axis=1,
        tiled=True,
    )
    grad_heads = grad_heads.reshape(images, full_len, local_heads, HEAD_DIM)

    def attend_back(inputs):
        single, grad_single, log_single = inputs
        queries, keys_in, values_in = (single[:, 0], single[:, 1], single[:, 2])
        scores = (
            jnp.einsum("qhd,khd->hqk", queries, keys_in, preferred_element_type=jnp.float32)
            * score_scale
        )
        probs = jnp.exp(scores - log_single[..., None])
        probs_low = probs.astype(jnp.bfloat16)
        grad_values = jnp.einsum(
            "hqk,qhd->khd", probs_low, grad_single, preferred_element_type=jnp.float32
        )
        grad_probs = jnp.einsum(
            "qhd,khd->hqk", grad_single, values_in, preferred_element_type=jnp.float32
        )
        grad_scores = probs * (grad_probs - jnp.sum(probs * grad_probs, axis=-1, keepdims=True))
        grad_scores = grad_scores.astype(jnp.bfloat16)
        grad_queries = (
            jnp.einsum("hqk,khd->qhd", grad_scores, keys_in, preferred_element_type=jnp.float32)
            * score_scale
        )
        grad_keys = (
            jnp.einsum("hqk,qhd->khd", grad_scores, queries, preferred_element_type=jnp.float32)
            * score_scale
        )
        return jnp.stack([grad_queries, grad_keys, grad_values], axis=1).astype(jnp.bfloat16)

    grad_joint_heads = lax.map(attend_back, (by_heads, grad_heads, log_total))
    grad_joint = lax.all_to_all(
        grad_joint_heads.reshape(images, full_len, 3, 1, head_block),
        "seq",
        split_axis=1,
        concat_axis=3,
        tiled=True,
    )
    grad_joint = grad_joint.reshape(row_count, 3 * features)
    joint_weight_grad = outer_sum(input_one, grad_joint)
    joint_sums = column_sums(grad_joint)
    query_bias_grad = joint_sums[:features]
    value_bias_grad = joint_sums[2 * features :]
    grad_in_one = back_product(grad_joint, joint_weight)
    attend_gain_grad = jnp.sum(grad_in_one * normed_one, axis=0)
    attend_shift_grad = jnp.sum(grad_in_one, axis=0)
    grad_embedded = grad_attn + normalize_back(grad_in_one, normed_one, scaling_one, gain_one)
    mask_token_grad = jnp.sum(jnp.where(masked[:, None], grad_embedded, 0.0), axis=0)
    patch_grad = jnp.where(masked[:, None], 0.0, grad_embedded).reshape(images, quarter, features)
    (
        attend_gain_grad,
        attend_shift_grad,
        joint_weight_grad,
        query_bias_grad,
        value_bias_grad,
        output_weight_grad,
        output_bias_grad,
        feed_gain_grad,
        feed_shift_grad,
        expand_weight_grad,
        expand_bias_grad,
        reduce_weight_grad,
        reduce_bias_grad,
        pixel_weight_grad,
        pixel_bias_grad,
        mask_token_grad,
    ) = (
        lax.psum_scatter(attend_gain_grad, "dp", scatter_dimension=0, tiled=True),
        lax.psum_scatter(attend_shift_grad, "dp", scatter_dimension=0, tiled=True),
        lax.psum_scatter(joint_weight_grad, "dp", scatter_dimension=0, tiled=True),
        lax.psum_scatter(query_bias_grad, "dp", scatter_dimension=0, tiled=True),
        lax.psum_scatter(value_bias_grad, "dp", scatter_dimension=0, tiled=True),
        lax.psum_scatter(output_weight_grad, "dp", scatter_dimension=0, tiled=True),
        lax.psum_scatter(output_bias_grad, "dp", scatter_dimension=0, tiled=True),
        lax.psum_scatter(feed_gain_grad, "dp", scatter_dimension=0, tiled=True),
        lax.psum_scatter(feed_shift_grad, "dp", scatter_dimension=0, tiled=True),
        lax.psum_scatter(expand_weight_grad, "dp", scatter_dimension=0, tiled=True),
        lax.psum_scatter(expand_bias_grad, "dp", scatter_dimension=0, tiled=True),
        lax.psum_scatter(reduce_weight_grad, "dp", scatter_dimension=0, tiled=True),
        lax.psum_scatter(reduce_bias_grad, "dp", scatter_dimension=0, tiled=True),
        lax.psum_scatter(pixel_weight_grad, "dp", scatter_dimension=0, tiled=True),
        lax.psum_scatter(pixel_bias_grad, "dp", scatter_dimension=0, tiled=True),
        lax.psum_scatter(mask_token_grad, "dp", scatter_dimension=0, tiled=True),
    )
    (
        attend_gain_grad,
        attend_shift_grad,
        joint_weight_grad,
        query_bias_grad,
        value_bias_grad,
        output_weight_grad,
        output_bias_grad,
        feed_gain_grad,
        feed_shift_grad,
        expand_weight_grad,
        expand_bias_grad,
        reduce_weight_grad,
        reduce_bias_grad,
        pixel_weight_grad,
        pixel_bias_grad,
        mask_token_grad,
    ) = (
        lax.psum(attend_gain_grad.astype(jnp.bfloat16), "seq").astype(jnp.float32),
        lax.psum(attend_shift_grad.astype(jnp.bfloat16), "seq").astype(jnp.float32),
        lax.psum(joint_weight_grad.astype(jnp.bfloat16), "seq").astype(jnp.float32),
        lax.psum(query_bias_grad.astype(jnp.bfloat16), "seq").astype(jnp.float32),
        lax.psum(value_bias_grad.astype(jnp.bfloat16), "seq").astype(jnp.float32),
        lax.psum(output_weight_grad.astype(jnp.bfloat16), "seq").astype(jnp.float32),
        lax.psum(output_bias_grad.astype(jnp.bfloat16), "seq").astype(jnp.float32),
        lax.psum(feed_gain_grad.astype(jnp.bfloat16), "seq").astype(jnp.float32),
        lax.psum(feed_shift_grad.astype(jnp.bfloat16), "seq").astype(jnp.float32),
        lax.psum(expand_weight_grad.astype(jnp.bfloat16), "seq").astype(jnp.float32),
        lax.psum(expand_bias_grad.astype(jnp.bfloat16), "seq").astype(jnp.float32),
        lax.psum(reduce_weight_grad.astype(jnp.bfloat16), "seq").astype(jnp.float32),
        lax.psum(reduce_bias_grad.astype(jnp.bfloat16), "seq").astype(jnp.float32),
        lax.psum(pixel_weight_grad.astype(jnp.bfloat16), "seq").astype(jnp.float32),
        lax.psum(pixel_bias_grad.astype(jnp.bfloat16), "seq").astype(jnp.float32),
        lax.psum(mask_token_grad.astype(jnp.bfloat16), "seq").astype(jnp.float32),
    )
    return (
        loss_value,
        attend_gain_grad,
        attend_shift_grad,
        joint_weight_grad,
        query_bias_grad,
        value_bias_grad,
        output_weight_grad,
        output_bias_grad,
        feed_gain_grad,
        feed_shift_grad,
        expand_weight_grad,
        expand_bias_grad,
        reduce_weight_grad,
        reduce_bias_grad,
        pixel_weight_grad,
        pixel_bias_grad,
        mask_token_grad,
        patch_grad,
    )


def solution(mesh):
    placed = (
        P("dp", "seq", None),
        P("dp", "seq", None),
        P("dp", "seq"),
        P("dp"),
        P(),
        P(),
        P(),
        P(),
        P(),
        P(),
        P(),
        P(),
        P(),
        P(),
        P(),
        P(),
        P(),
        P(),
        P(),
        P(),
    )
    return jax.shard_map(
        on_device,
        mesh=mesh,
        in_specs=placed,
        out_specs=(
            P(),
            P("dp"),
            P("dp"),
            P("dp", None),
            P("dp"),
            P("dp"),
            P("dp", None),
            P("dp"),
            P("dp"),
            P("dp"),
            P("dp", None),
            P("dp"),
            P("dp", None),
            P("dp"),
            P("dp", None),
            P("dp"),
            P("dp"),
            P("dp", "seq", None),
        ),
        check_vma=False,
    )
```

profile of v0, /device:TPU:0, one launch (start us, length us, event | category | flops | bytes accessed | tf_op | source)
XLA Modules:
  0.0 1127.7 jit_solution(12987718975133235999)
XLA Ops:
  21.8 3.0 add_convert_fusion.5
  24.9 4.7 add_convert_fusion.1
  29.6 10.9 reshape.276
  40.5 5.6 copy.82
  46.1 5.1 all-to-all-start
  51.2 60.8 %all-to-all-done = bf16[6,144,3,4,192]{4,1,2,0,3:T(8,128)(2,1)} async-done(((bf16[6,144,3,4,192]{4,1,2,0,3:T(8,128)(2,1)}), bf16[6,144,3,4,192]{4,1,2,0,3:T(8,128)(2,1)}, u32[]{:S(2)}, u32[]{:S(2)}) %all-to-all-start) | async-done | bytes 3981344 | tf_op jit(solution)/shard_map/all_to_all | solution.py:90
  111.9 13.6 %copy.83 = bf16[6,4,144,3,1,192]{2,1,5,3,0,4:T(4,128)(2,1)} copy(bf16[6,4,144,3,1,192]{5,2,3,0,1,4:T(8,128)(2,1)} %bitcast.21) | data formatting | bytes 7962624 | tf_op jit(solution)/shard_map/all_to_all | solution.py:90
  125.5 12.5 %reshape.277 = bf16[6,576,3,3,64]{1,4,3,2,0:T(8,128)(2,1)} reshape(bf16[6,4,144,3,1,192]{2,1,5,3,0,4:T(4,128)(2,1)} %copy.83) | data formatting | bytes 7962624 | tf_op jit(solution)/shard_map/reshape | solution.py:91
  138.1 30.8 %while.22 = (s32[]{:T(128)}, bf16[6,576,3,64]{1,3,2,0:T(8,128)(2,1)}, f32[6,3,576]{2,1,0:T(4,128)}, bf16[6,576,3,3,64]{1,4,3,2,0:T(8,128)(2,1)}, s32[]{:T(128)}) while((s32[]{:T(128)}, bf16[6,576,3,64]{1,3,2,0:T(8,128)(2,1)}, f32[6,3,576]{2,1,0:T(4,128)}, bf16[6,576,3,3,64]{1,4,3,2,0:T(8,128)(2,1)}, s32[]{:T(128)}) %tuple.62), condition=%wide.region_5.6_spmd, body=%wide.region_2.5_spmd.sunk | while | flops 263870784 | bytes 14761809 | solution.py:106
  168.9 4.6 copy.84
  173.5 4.6 all-to-all-start.1
  184.5 22.2 %all-to-all-done.1 = bf16[6,576,1,192]{3,0,2,1:T(8,128)(2,1)} async-done(((bf16[6,576,1,192]{3,0,2,1:T(8,128)(2,1)}), bf16[6,576,1,192]{3,0,2,1:T(8,128)(2,1)}, u32[]{:S(2)}, u32[]{:S(2)}) %all-to-all-start.1) | async-done | bytes 1327136 | tf_op jit(solution)/shard_map/all_to_all | solution.py:107
  210.9 4.3 reshape.279
  215.2 4.0 fusion.50
  220.6 29.2 %multiply_convert_fusion.1 = (bf16[864,3072]{1,0:T(8,128)(2,1)S(1)}, f32[864,3072]{1,0:T(8,128)}, f32[864,3072]{1,0:T(8,128)}) fusion(f32[3072]{0:T(1024)S(1)} %copy-done.23, bf16[768,3072]{1,0:T(8,128)(2,1)S(1)} %bitcast.171, f32[864,768]{1,0:T(8,128)S(1)} %get-tuple-element.146, f32[768]{0:T(1024)S(1)} %convert_element_type.242, ...), kind=kOutput, calls=%fused_computation.50 | convolution fusion | flops 4255358976 | bytes 33940224 | tf_op jit(solution)/shard_map/dot_general | solution.py:123
  249.8 4.3 add_convert_fusion.3
  254.2 4.3 multiply_reduce_fusion.6
  258.5 40.9 %all-reduce.11 = (f32[768]{0:T(1024)}, f32[]{:T(128)}) all-reduce(f32[768]{0:T(1024)} %get-tuple-element.148, f32[]{:T(128)} %get-tuple-element.132), channel_id=1, replica_groups=mesh['dp'=8,'seq'=4] {'dp','seq'}, use_global_device_ids=true, to_apply=%region_9.10 | all-reduce | flops 769 | bytes 6152 | tf_op jit(solution)/shard_map/psum | solution.py:140
  300.0 3.7 convert_reduce_fusion.2
  307.7 4.4 fusion.51
  312.1 15.5 %convert_reduce_fusion = (f32[3072]{0:T(1024)}, bf16[864,3072]{1,0:T(8,128)(2,1)}) fusion(f32[864,3072]{1,0:T(8,128)} %get-tuple-element.135, bf16[3072,768]{1,0:T(8,128)(2,1)} %param.39, f32[864,768]{1,0:T(8,128)} %fusion.51, f32[864,3072]{1,0:T(8,128)} %get-tuple-element.147, f32[3072]{0:T(1024)} %convert_element_type.244), kind=kOutput, calls=%fused_computation.47 | convolution fusion | flops 4122645504 | bytes 33939456 | tf_op jit(solution)/shard_map/rb,ab->ra/dot_general | solution.py:33
  327.6 9.6 multiply_reduce_fusion.3
  343.2 4.9 reshape.280
  348.1 2.9 copy.87
  351.0 4.4 all-to-all-start.2
  355.5 5.0 fusion.37
  360.4 17.2 %all-to-all-done.2 = bf16[6,144,4,192]{3,1,0,2:T(8,128)(2,1)} async-done(((bf16[6,144,4,192]{3,1,0,2:T(8,128)(2,1)}), bf16[6,144,4,192]{3,1,0,2:T(8,128)(2,1)}, u32[]{:S(2)}, u32[]{:S(2)}) %all-to-all-start.2) | async-done | bytes 1327136 | tf_op jit(solution)/shard_map/all_to_all | solution.py:161
  377.7 5.3 copy.88
  383.0 5.0 reshape.281
  387.9 59.4 %while.23 = (s32[]{:T(128)}, bf16[6,576,3,3,64]{1,4,3,2,0:T(8,128)(2,1)}, bf16[6,576,3,3,64]{1,4,3,2,0:T(8,128)(2,1)}, f32[6,3,576]{2,1,0:T(4,128)}, bf16[6,576,3,64]{1,3,2,0:T(8,128)(2,1)}, /*index=5*/s32[]{:T(128)}) while((s32[]{:T(128)}, bf16[6,576,3,3,64]{1,4,3,2,0:T(8,128)(2,1)}, bf16[6,576,3,3,64]{1,4,3,2,0:T(8,128)(2,1)}, ...), condition=%wide.region_17.18_spmd, body=%wide.region_15.17_spmd.sunk | while | flops 651495744 | bytes 35908192 | solution.py:197
  447.4 10.5 copy.89
  457.9 5.6 all-to-all-start.3
  463.6 3.2 add_convert_fusion.2
  466.7 75.9 %all-to-all-done.3 = bf16[6,576,3,1,192]{4,0,3,2,1:T(8,128)(2,1)} async-done(((bf16[6,576,3,1,192]{4,0,3,2,1:T(8,128)(2,1)}), bf16[6,576,3,1,192]{4,0,3,2,1:T(8,128)(2,1)}, u32[]{:S(2)}, u32[]{:S(2)}) %all-to-all-start.3) | async-done | bytes 3981344 | tf_op jit(solution)/shard_map/all_to_all | solution.py:198
  542.6 4.2 copy.90
  549.1 5.0 copy.91
  554.2 9.8 reshape.283
  564.0 9.3 fusion.52
  573.3 10.7 fusion.46
  584.2 10.2 fusion.40
  598.2 3.5 convert_reduce_fusion.1
  605.0 9.3 multiply_reduce_fusion.2
  618.2 84.0 %reduce-scatter.6.cloned.1.call-done = f32[96,2304]{1,0:T(8,128)} async-done(((f32[768,2304]{1,0:T(8,128)}), f32[96,2304]{1,0:T(8,128)}) %reduce-scatter.6.cloned.1.call-update) | async-done | bytes 884752 | tf_op jit(solution)/shard_map/reduce_scatter | solution.py:236
  704.2 164.5 %reduce-scatter.10.cloned.1.call-done = f32[96,3072]{1,0:T(8,128)} async-done(((f32[768,3072]{1,0:T(8,128)}), f32[96,3072]{1,0:T(8,128)}) %reduce-scatter.10.cloned.1.call-update) | async-done | bytes 1179664 | tf_op jit(solution)/shard_map/reduce_scatter | solution.py:243
  870.8 164.3 %reduce-scatter.12.cloned.1.call-done = f32[384,768]{1,0:T(8,128)} async-done(((f32[3072,768]{1,0:T(8,128)}), f32[384,768]{1,0:T(8,128)}) %reduce-scatter.12.cloned.1.call-update) | async-done | bytes 1179664 | tf_op jit(solution)/shard_map/reduce_scatter | solution.py:245
  1037.9 4.8 broadcast_select_fusion
  1043.4 36.7 %all-reduce.12 = (bf16[768]{0:T(1024)(128)(2,1)}, bf16[768]{0:T(1024)(128)(2,1)}, bf16[768]{0:T(1024)(128)(2,1)}, bf16[768]{0:T(1024)(128)(2,1)}, bf16[768]{0:T(...) all-reduce(f32[768]{0:T(1024)} %get-tuple-element.74, ...), channel_id=2, replica_groups=mesh['dp'=8,'seq'=4] {'dp'}, use_global_device_ids=true, to_apply=%region_19.20.clone | all-reduce | flops 10752 | bytes 64512
  1092.4 6.5 all-reduce.13
  (253 shorter events, 178.4 us)
Async XLA Ops:
  7.2 17.7 %copy-start = (bf16[768,2304]{1,0:T(8,128)(2,1)S(1)}, bf16[768,2304]{1,0:T(8,128)(2,1)}, u32[]{:S(2)}) copy-start(bf16[768,2304]{1,0:T(8,128)(2,1)} %param.30) | copy-start | bytes 10616836
  8.7 3.9 copy-start.14
  10.1 14.8 %copy-start.8 = (f32[768]{0:T(1024)}, f32[768]{0:T(1024)S(1)}, u32[]{:S(2)}) copy-start(f32[768]{0:T(1024)S(1)} %convert_element_type.230) | copy-start | bytes 9220
  11.9 12.9 %copy-start.10 = (f32[6,144]{1,0:T(8,128)}, f32[6,144]{1,0:T(8,128)S(1)}, u32[]{:S(2)}) copy-start(f32[6,144]{1,0:T(8,128)S(1)} %broadcast_multiply_fusion) | copy-start | bytes 10372
  15.3 9.5 copy-start.12
  46.1 65.8 %all-to-all-start = ((bf16[6,144,3,4,192]{4,1,2,0,3:T(8,128)(2,1)}), bf16[6,144,3,4,192]{4,1,2,0,3:T(8,128)(2,1)}, u32[]{:S(2)}, u32[]{:S(2)}) async-start(bf16[6,144,3,4,192]{4,1,2,0,3:T(8,128)(2,1)} %copy.82), calls=%async_computation | async-start | bytes 10616832 | tf_op jit(solution)/shard_map/all_to_all | solution.py:90
  173.5 5.2 copy-start.17
  173.5 5.8 copy-start.27
  173.5 33.2 %all-to-all-start.1 = ((bf16[6,576,1,192]{3,0,2,1:T(8,128)(2,1)}), bf16[6,576,1,192]{3,0,2,1:T(8,128)(2,1)}, u32[]{:S(2)}, u32[]{:S(2)}) async-start(bf16[6,576,1,192]{3,0,2,1:T(8,128)(2,1)} %copy.84), calls=%async_computation.1 | async-start | bytes 4718592 | tf_op jit(solution)/shard_map/all_to_all | solution.py:107
  178.2 436.7 %reduce-scatter.14.cloned.1.call-start = ((), (), s32[]{:S(2)}) async-start(), calls=%async_computation.13 | async-start | bytes 2654208 | tf_op jit(solution)/shard_map/reduce_scatter | solution.py:247
  180.0 39.7 %copy-start.11 = (f32[768]{0:T(1024)}, f32[768]{0:T(1024)S(1)}, u32[]{:S(2)}) copy-start(f32[768]{0:T(1024)S(1)} %convert_element_type.242) | copy-start | bytes 9220
  215.2 4.5 slice-start.2
  215.2 4.5 slice-start.3
  215.2 34.5 %slice-start = ((s8[4718592]{0:T(1024)(128)(4,1)}), s8[4194304]{0:T(1024)(128)(4,1)S(1)}, s32[]{:S(2)}) async-start(s8[4718592]{0:T(1024)(128)(4,1)} %bitcast.168), calls=%async_computation.15 | async-start | bytes 8388608
  219.2 30.6 %copy-start.2 = (f32[864,768]{1,0:T(8,128)}, f32[864,768]{1,0:T(8,128)S(1)}, u32[]{:S(2)}) copy-start(f32[864,768]{1,0:T(8,128)S(1)} %get-tuple-element.146) | copy-start | bytes 7962628
  219.2 1.4 copy-start.23
  220.6 29.2 %copy-start.26 = (f32[768]{0:T(1024)S(1)}, f32[768]{0:T(1024)}, u32[]{:S(2)}) copy-start(f32[768]{0:T(1024)} %convert_element_type.246) | copy-start | bytes 9220
  220.6 29.2 %slice-start.1 = ((s8[4718592]{0:T(1024)(128)(4,1)}), s8[524288]{0:T(1024)(128)(4,1)S(1)}, s32[]{:S(2)}) async-start(s8[4718592]{0:T(1024)(128)(4,1)} %bitcast.168), calls=%async_computation.16 | async-start | bytes 1048576
  249.8 4.4 copy-start.34
  249.8 4.4 copy-start.22
  249.8 4.4 copy-start.25
  249.8 4.4 copy-start.28
  249.8 4.4 copy-start.29
  254.1 4.3 copy-start.32
  300.0 4.8 copy-start.33
  303.8 1.1 copy-start.6
  312.1 15.6 %copy-start.3 = (f32[864,768]{1,0:T(8,128)S(1)}, f32[864,768]{1,0:T(8,128)}, u32[]{:S(2)}) copy-start(f32[864,768]{1,0:T(8,128)} %copy-done.2) | copy-start | bytes 7962628
  327.6 9.6 copy-start.5
  337.3 3.6 copy-start.30
  339.3 1.5 copy-start.4
  351.0 26.6 %all-to-all-start.2 = ((bf16[6,144,4,192]{3,1,0,2:T(8,128)(2,1)}), bf16[6,144,4,192]{3,1,0,2:T(8,128)(2,1)}, u32[]{:S(2)}, u32[]{:S(2)}) async-start(bf16[6,144,4,192]{3,1,0,2:T(8,128)(2,1)} %copy.87), calls=%async_computation.2 | async-start | bytes 3538944 | tf_op jit(solution)/shard_map/all_to_all | solution.py:161
  355.4 261.1 %reduce-scatter.8.cloned.1.call-start = ((), (), s32[]{:S(2)}) async-start(), calls=%async_computation.10 | async-start | bytes 2654208 | tf_op jit(solution)/shard_map/reduce_scatter | solution.py:239
  457.9 5.7 copy-start.9
  457.9 84.7 %all-to-all-start.3 = ((bf16[6,576,3,1,192]{4,0,3,2,1:T(8,128)(2,1)}), bf16[6,576,3,1,192]{4,0,3,2,1:T(8,128)(2,1)}, u32[]{:S(2)}, u32[]{:S(2)}) async-start(bf16[6,576,3,1,192]{4,0,3,2,1:T(8,128)(2,1)} %copy.89), calls=%async_computation.3 | async-start | bytes 14155776 | tf_op jit(solution)/shard_map/all_to_all | solution.py:198
  463.5 238.7 %reduce-scatter.6.cloned.1.call-start = ((), (), s32[]{:S(2)}) async-start(), calls=%async_computation.9 | async-start | bytes 7962624 | tf_op jit(solution)/shard_map/reduce_scatter | solution.py:236
  546.8 2.3 copy-start.1
  573.3 295.3 %reduce-scatter.10.cloned.1.call-start = ((), (), s32[]{:S(2)}) async-start(), calls=%async_computation.11 | async-start | bytes 10616832 | tf_op jit(solution)/shard_map/reduce_scatter | solution.py:243
  584.1 451.0 %reduce-scatter.12.cloned.1.call-start = ((), (), s32[]{:S(2)}) async-start(), calls=%async_computation.12 | async-start | bytes 10616832 | tf_op jit(solution)/shard_map/reduce_scatter | solution.py:245
  594.4 2.5 copy-start.24
  594.4 516.5 %all-reduce.17.cloned.1.call-start = ((), (), s32[]{:S(2)}) async-start(), calls=%async_computation.14 | async-start | bytes 3833856 | tf_op jit(solution)/shard_map/psum | solution.py:271
  598.2 6.8 copy-start.13
  598.2 6.8 copy-start.15
  598.2 6.8 copy-start.16
  1037.9 4.8 copy-start.18
  1042.7 0.7 copy-start.19
  1042.7 0.7 copy-start.20
  1042.7 0.7 copy-start.21
  1110.9 7.5 copy-start.7
  (1 other events, 0.7 us)
Sparse Core Ops, SparseCore 0:
  312.2 69.9 reduce-scatter.13
  385.7 68.0 reduce-scatter.7
  573.4 128.7 reduce-scatter.5
  706.1 162.5 reduce-scatter.9
  872.5 162.5 reduce-scatter.11
  1039.0 48.4 all-reduce.16
where the time goes:
time: 1140 us; the launch traced here: 1130 us
  waiting for transfers between devices  589 us (52%)
  matrix products  177 us (16%)
  local copies, waits for them, and re-layouts  148 us (13%)
  other arithmetic  91 us (8%)
  blocking collectives  84.1 us (7%)
  starting transfers between devices  20.4 us (2%)
  between operations  18.5 us (2%)
    reduce_scatter x1, waiting for transfers between devices, on_device(): lax.psum_scatter(expand_weight_grad, 'dp', scatter_dimension=0, tiled=True)  164 us
    reduce_scatter x1, waiting for transfers between devices, on_device(): lax.psum_scatter(reduce_weight_grad, 'dp', scatter_dimension=0, tiled=True)  164 us
    reduce_scatter x1, waiting for transfers between devices, on_device(): lax.psum_scatter(joint_weight_grad, 'dp', scatter_dimension=0, tiled=True)  84 us
    all_to_all x1, waiting for transfers between devices, on_device(): lax.all_to_all(grad_joint_heads.reshape(images, full_len, 3, 1, head_bloc...  75.9 us
    all_to_all x1, waiting for transfers between devices, on_device(): lax.all_to_all(joint, 'seq', split_axis=3, concat_axis=1, tiled=True)  60.8 us
    dot_general x5, matrix products, back_product(): jnp.einsum('rb,ab->ra', left, right, preferred_element_type=jnp.float32)  41.2 us
    psum x1, blocking collectives, on_device(): lax.psum((channel_sums, jnp.sum(mask_float)), ('dp', 'seq'))  40.9 us
    dot_general x5, matrix products, outer_sum(): jnp.einsum('ra,rb->ab', left, right, preferred_element_type=jnp.float32)  38.1 us
  transfers between devices with their start and end apart: 10, of which 7 were waited for; matrix products, arithmetic and copies ran while one was open for 21% of the time, Pallas kernels for 0%

commit v1 on v0

v1 whole, which is shorter than its diff:
```python
import functools
import itertools
from functools import partial

import jax
import jax.numpy as jnp
from jax import lax
from jax.experimental import pallas as pl
from jax.experimental.pallas import tpu as pltpu
from jax.sharding import PartitionSpec as P

HEADS = 12
HEAD_DIM = 64
PIXELS = 768
WIDE = 768
PAIR = 2 * HEAD_DIM
MIB = 1 << 20
F32 = jnp.float32
BF16 = jnp.bfloat16


def dot(left, right):
    return jnp.dot(left, right, preferred_element_type=F32)


def dot_nt(left, right):
    return lax.dot_general(left, right, (((1,), (1,)), ((), ())), preferred_element_type=F32)


def dot_tn(left, right):
    return lax.dot_general(left, right, (((0,), (0,)), ((), ())), preferred_element_type=F32)


def normalize(inputs):
    centre = inputs - jnp.mean(inputs, axis=-1, keepdims=True)
    scaling = lax.rsqrt(jnp.mean(centre * centre, axis=-1, keepdims=True) + 1e-06)
    return (centre * scaling, scaling)


def normalize_back(upstream, normed, scaling, gain):
    scaled = upstream * gain
    return scaling * (
        scaled
        - jnp.mean(scaled, axis=-1, keepdims=True)
        - normed * jnp.mean(scaled * normed, axis=-1, keepdims=True)
    )


def column_sums(values):
    return jnp.sum(values.astype(F32), axis=0, keepdims=True)


def gelu_both(inputs):
    bell = jnp.exp(inputs * inputs * -0.5)
    base_of = 1.0 + (0.3275911 * 0.7071067811865476) * jnp.abs(inputs)
    inner = pl.reciprocal(base_of, approx=True)
    inner = inner * (2.0 - base_of * inner)
    series = inner * (
        0.254829592
        + inner * (-0.284496736 + inner * (1.421413741 + inner * (-1.453152027 + inner * 1.061405429)))
    )
    tail = 0.5 * series * bell
    below = jnp.where(inputs < 0.0, tail, 1.0 - tail)
    return (inputs * below, below + inputs * bell * 0.3989422804014327)


def params(limit):
    return pltpu.CompilerParams(vmem_limit_bytes=limit * MIB)


def fixed(shape):
    zeros = (0,) * len(shape)
    return pl.BlockSpec(shape, lambda *place: zeros, pipeline_mode=pl.Buffered(1))


def cost(flops, moved):
    return pl.CostEstimate(flops=int(flops), bytes_accessed=int(moved), transcendentals=0)


def project_kernel(own, far, gain, shift, weight, bias, embedded_out, joint_out):
    embedded = jnp.concatenate([own[0], far[0]], axis=0)
    embedded_out[0] = embedded
    normed, _ = normalize(embedded.astype(F32))
    low = (normed * gain[...] + shift[...]).astype(BF16)
    for part in range(3):
        cut = slice(part * WIDE, (part + 1) * WIDE)
        joint_out[0, part] = (dot(low, weight[:, cut]) + bias[:, cut]).astype(BF16)


def project(own, far, gain, shift, weight, bias):
    near, quarter, width = own.shape
    rows = 2 * quarter
    return pl.pallas_call(
        project_kernel,
        grid=(near,),
        in_specs=[
            pl.BlockSpec((1, quarter, width), lambda i: (i, 0, 0)),
            pl.BlockSpec((1, quarter, width), lambda i: (i, 0, 0)),
            fixed((1, width)),
            fixed((1, width)),
            fixed((width, 3 * width)),
            fixed((1, 3 * width)),
        ],
        out_specs=[
            pl.BlockSpec((1, rows, width), lambda i: (i, 0, 0)),
            pl.BlockSpec((1, 3, rows, width), lambda i: (i, 0, 0, 0)),
        ],
        out_shape=[
            jax.ShapeDtypeStruct((near, rows, width), BF16),
            jax.ShapeDtypeStruct((near, 3, rows, width), BF16),
        ],
        compiler_params=params(32),
        cost_estimate=cost(2 * near * rows * width * 3 * width, 12e6),
        name="project",
    )(own, far, gain, shift, weight, bias)


def side_by_side(pair):
    lanes = lax.broadcasted_iota(jnp.int32, pair.shape, 1)
    zero = jnp.zeros_like(pair)
    first = jnp.where(lanes < HEAD_DIM, pair, zero)
    second = jnp.where(lanes < HEAD_DIM, zero, pair)
    return jnp.concatenate([first, second], axis=0)


def merge_heads(stacked):
    rows = stacked.shape[0] // 2
    lanes = lax.broadcasted_iota(jnp.int32, (rows, PAIR), 1)
    return jnp.where(lanes < HEAD_DIM, stacked[:rows], stacked[rows:])


def attend_kernel(own, far, mixed_out, probs_out):
    queries = side_by_side(own[0, 0] * jnp.asarray(HEAD_DIM**-0.5, BF16))
    keys_in = jnp.concatenate([own[0, 1], far[0, 0]], axis=0)
    values_in = jnp.concatenate([own[0, 2], far[0, 1]], axis=0)
    scores = dot_nt(queries, keys_in)
    exponent = jnp.exp(scores - jnp.max(scores, axis=-1, keepdims=True))
    total = jnp.sum(exponent, axis=-1, keepdims=True)
    probs = (exponent * (1.0 / total)).astype(BF16)
    probs_out[0, 0] = probs
    mixed_out[0] = merge_heads(dot(probs, values_in)).astype(BF16)


def attend(joint, pairs_far):
    near, _, rows, width = joint.shape
    keys_count = 2 * rows
    pairs = width // PAIR
    return pl.pallas_call(
        attend_kernel,
        grid=(near, pairs),
        in_specs=[
            pl.BlockSpec((1, 3, rows, PAIR), lambda i, h: (i, 0, 0, h)),
            pl.BlockSpec((1, 2, rows, PAIR), lambda i, h: (i, 0, 0, h)),
        ],
        out_specs=[
            pl.BlockSpec((1, rows, PAIR), lambda i, h: (i, 0, h)),
            pl.BlockSpec((1, 1, 2 * rows, keys_count), lambda i, h: (i, h, 0, 0)),
        ],
        out_shape=[
            jax.ShapeDtypeStruct((near, rows, width), BF16),
            jax.ShapeDtypeStruct((near, pairs, 2 * rows, keys_count), BF16),
        ],
        compiler_params=params(32),
        cost_estimate=cost(8 * near * rows * keys_count * width, 20e6),
        name="attend",
    )(joint, pairs_far)


def attend_back_kernel(own, far, probs_in, upstream, query_out, own_out, far_out):
    rows = own.shape[2]
    scale = HEAD_DIM**-0.5
    queries = side_by_side(own[0, 0])
    keys_in = jnp.concatenate([own[0, 1], far[0, 0]], axis=0)
    values_in = jnp.concatenate([own[0, 2], far[0, 1]], axis=0)
    grad_mixed = side_by_side(upstream[0])
    probs = probs_in[0, 0]
    grad_probs = dot_nt(grad_mixed, values_in)
    wide = probs.astype(F32)
    weighted = wide * grad_probs
    inner = jnp.sum(weighted, axis=-1, keepdims=True)
    grad_scores = (weighted - wide * inner).astype(BF16)
    query_out[0] = (merge_heads(dot(grad_scores, keys_in)) * scale).astype(BF16)
    grad_values = dot_tn(probs, grad_mixed).astype(BF16)
    grad_keys = (dot_tn(grad_scores, queries) * scale).astype(BF16)
    own_out[0, 0] = grad_keys[:rows]
    own_out[0, 1] = grad_values[:rows]
    far_out[0, 0] = grad_keys[rows:]
    far_out[0, 1] = grad_values[rows:]


def attend_back(joint, pairs_far, probs, upstream):
    near, _, rows, width = joint.shape
    keys_count = 2 * rows
    pairs = width // PAIR
    two = pl.BlockSpec((1, 2, rows, PAIR), lambda i, h: (i, 0, 0, h))
    one = pl.BlockSpec((1, rows, PAIR), lambda i, h: (i, 0, h))
    return pl.pallas_call(
        attend_back_kernel,
        grid=(near, pairs),
        in_specs=[
            pl.BlockSpec((1, 3, rows, PAIR), lambda i, h: (i, 0, 0, h)),
            two,
            pl.BlockSpec((1, 1, 2 * rows, keys_count), lambda i, h: (i, h, 0, 0)),
            one,
        ],
        out_specs=[one, two, two],
        out_shape=[
            jax.ShapeDtypeStruct((near, rows, width), BF16),
            jax.ShapeDtypeStruct((near, 2, rows, width), BF16),
            jax.ShapeDtypeStruct((near, 2, rows, width), BF16),
        ],
        compiler_params=params(32),
        cost_estimate=cost(16 * near * rows * keys_count * width, 25e6),
        name="attend_back",
    )(joint, pairs_far, probs, upstream)


def rows_kernel(
    hidden,
    inverse,
    embedded_in,
    mixed,
    mask_in,
    target_own,
    target_far,
    output_weight,
    expand_weight,
    reduce_weight,
    pixel_weight,
    biases,
    expand_bias,
    input_out,
    active_out,
    after_out,
    pred_out,
    branch_out,
    expand_out,
    low_out,
    attn_out,
    mixed_out,
    sums_out,
    slope,
):
    output_bias, gain, shift, reduce_bias, pixel_bias = (biases[row : row + 1] for row in range(5))
    mask = mask_in[0]
    after_attn = embedded_in[0].astype(F32) + dot(mixed[0], output_weight[...]) + output_bias
    normed, scaling = normalize(after_attn)
    low = (normed * gain + shift).astype(BF16)
    input_out[0] = low
    total = after_attn + reduce_bias
    for start in range(0, hidden, WIDE):
        cut = slice(start, start + WIDE)
        active, rate = gelu_both(dot(low, expand_weight[:, cut]) + expand_bias[:, cut])
        active = active.astype(BF16)
        active_out[0, :, cut] = active
        slope[:, cut] = rate.astype(slope.dtype)
        total += dot(active, reduce_weight[cut, :])
    after_low = total.astype(BF16)
    after_out[0] = after_low
    target = jnp.concatenate([target_own[0], target_far[0]], axis=0).astype(F32)
    errors = dot(after_low, pixel_weight[...]) + pixel_bias - target
    square = errors * errors + 1.0
    root = lax.rsqrt(square)
    channel = jnp.sum((square * root - 1.0) * mask, axis=0, keepdims=True)
    grad_pred = (mask * errors * root * inverse[0, 0]).astype(BF16)
    pred_out[0] = grad_pred
    grad_mlp = dot_nt(grad_pred, pixel_weight[...])
    branch = grad_mlp.astype(BF16)
    branch_out[0] = branch
    grad_in = jnp.zeros_like(grad_mlp)
    expand_sums = []
    for start in range(0, hidden, WIDE):
        cut = slice(start, start + WIDE)
        grad_expand = dot_nt(branch, reduce_weight[cut, :]) * slope[:, cut].astype(F32)
        grad_expand = grad_expand.astype(BF16)
        expand_out[0, :, cut] = grad_expand
        expand_sums.append(column_sums(grad_expand))
        grad_in += dot_nt(grad_expand, expand_weight[:, cut])
    grad_attn = grad_mlp + normalize_back(grad_in, normed, scaling, gain)
    attn_out[0] = grad_attn
    grad_low = grad_attn.astype(BF16)
    low_out[0] = grad_low
    mixed_out[0] = dot_nt(grad_low, output_weight[...]).astype(BF16)
    sums = [
        column_sums(grad_pred),
        column_sums(branch),
        column_sums(grad_in * normed),
        column_sums(grad_in),
        column_sums(grad_low),
        channel,
    ] + expand_sums

    @pl.when(pl.program_id(0) == 0)
    def _():
        sums_out[...] = jnp.zeros_like(sums_out)

    for row, line in enumerate(sums):
        sums_out[row : row + 1] += line


def rows_step(
    inverse,
    embedded,
    mixed,
    mask,
    target_own,
    target_far,
    output_weight,
    expand_weight,
    reduce_weight,
    pixel_weight,
    biases,
    expand_bias,
):
    near, rows, width = embedded.shape
    quarter = target_own.shape[1]
    hidden = expand_weight.shape[1]
    block = pl.BlockSpec((1, rows, width), lambda i: (i, 0, 0))
    half = pl.BlockSpec((1, quarter, width), lambda i: (i, 0, 0))
    long = pl.BlockSpec((1, rows, hidden), lambda i: (i, 0, 0))
    narrow = jax.ShapeDtypeStruct((near, rows, width), BF16)
    broad = jax.ShapeDtypeStruct((near, rows, hidden), BF16)
    return pl.pallas_call(
        partial(rows_kernel, hidden),
        grid=(near,),
        in_specs=[
            pl.BlockSpec(memory_space=pltpu.SMEM),
            block,
            block,
            pl.BlockSpec((1, rows, 1), lambda i: (i, 0, 0)),
            half,
            half,
            fixed((width, width)),
            fixed((width, hidden)),
            fixed((hidden, width)),
            fixed((width, width)),
            fixed((8, width)),
            fixed((1, hidden)),
        ],
        out_specs=[block, long, block, block, block, long, block, block, block, fixed_out((16, width))],
        out_shape=[
            narrow,
            broad,
            narrow,
            narrow,
            narrow,
            broad,
            narrow,
            jax.ShapeDtypeStruct((near, rows, width), F32),
            narrow,
            jax.ShapeDtypeStruct((16, width), F32),
        ],
        scratch_shapes=[pltpu.VMEM((rows, hidden), F32)],
        compiler_params=params(56),
        cost_estimate=cost(4 * near * rows * width * (2 * width + 2 * hidden), 40e6),
        name="rows_step",
    )(
        inverse,
        embedded,
        mixed,
        mask,
        target_own,
        target_far,
        output_weight,
        expand_weight,
        reduce_weight,
        pixel_weight,
        biases,
        expand_bias,
    )


def fixed_out(shape):
    zeros = (0,) * len(shape)
    return pl.BlockSpec(shape, lambda *place: zeros)


def outer_kernel(left_moves, left, right, out, turned):
    if left_moves:
        out[...] = dot_tn(left[...], right[...]).astype(out.dtype)
        return

    @pl.when(pl.program_id(0) == 0)
    def _():
        turned[...] = left[...].T

    out[...] = dot(turned[...], right[...]).astype(out.dtype)


def outer(left, right):
    rows, tall = left.shape
    broad = right.shape[1]
    left_moves = tall > broad
    if left_moves:
        grid, specs = tall // WIDE, [
            pl.BlockSpec((rows, WIDE), lambda i: (0, i)),
            fixed((rows, broad)),
        ]
        out_spec = pl.BlockSpec((WIDE, broad), lambda i: (i, 0))
    else:
        grid, specs = broad // WIDE, [
            fixed((rows, tall)),
            pl.BlockSpec((rows, WIDE), lambda i: (0, i)),
        ]
        out_spec = pl.BlockSpec((tall, WIDE), lambda i: (0, i))
    return pl.pallas_call(
        partial(outer_kernel, left_moves),
        grid=(grid,),
        in_specs=specs,
        out_specs=out_spec,
        out_shape=jax.ShapeDtypeStruct((tall, broad), BF16),
        scratch_shapes=[pltpu.VMEM((WIDE, rows), BF16)],
        compiler_params=params(32),
        cost_estimate=cost(2 * rows * tall * broad, 2 * (rows * (tall + broad) + tall * broad)),
        name="outer",
    )(left, right)


def project_back_kernel(
    query, own, received, embedded_in, attn, mask_in, gain, shift, weight,
    input_out, joint_out, near_out, far_out, sums_out,
):
    quarter = near_out.shape[1]
    mask = mask_in[0]
    embedded = embedded_in[0].astype(F32)
    normed, scaling = normalize(embedded)
    input_out[0] = (normed * gain[...] + shift[...]).astype(BF16)
    grad_query = query[0]
    grad_key = (own[0, 0].astype(F32) + received[0, 0].astype(F32)).astype(BF16)
    grad_value = (own[0, 1].astype(F32) + received[0, 1].astype(F32)).astype(BF16)
    grad_in = None
    for part, grad in enumerate((grad_query, grad_key, grad_value)):
        joint_out[part, 0] = grad
        term = dot_nt(grad, weight[:, part * WIDE : (part + 1) * WIDE])
        grad_in = term if grad_in is None else grad_in + term
    grad_embedded = attn[0] + normalize_back(grad_in, normed, scaling, gain[...])
    kept = grad_embedded * (1.0 - mask)
    near_out[0] = kept[:quarter]
    far_out[0] = kept[quarter:].astype(BF16)
    sums = [
        column_sums(grad_in * normed),
        column_sums(grad_in),
        column_sums(grad_query),
        column_sums(grad_value),
        column_sums(grad_embedded * mask),
    ]

    @pl.when(pl.program_id(0) == 0)
    def _():
        sums_out[...] = jnp.zeros_like(sums_out)

    for row, line in enumerate(sums):
        sums_out[row : row + 1] += line


def project_back(query, own, received, embedded, attn, mask, gain, shift, weight):
    near, rows, width = embedded.shape
    quarter = rows // 2
    block = pl.BlockSpec((1, rows, width), lambda i: (i, 0, 0))
    half = pl.BlockSpec((1, quarter, width), lambda i: (i, 0, 0))
    two = pl.BlockSpec((1, 2, rows, width), lambda i: (i, 0, 0, 0))
    return pl.pallas_call(
        project_back_kernel,
        grid=(near,),
        in_specs=[
            block,
            two,
            two,
            block,
            block,
            pl.BlockSpec((1, rows, 1), lambda i: (i, 0, 0)),
            fixed((1, width)),
            fixed((1, width)),
            fixed((width, 3 * width)),
        ],
        out_specs=[
            block,
            pl.BlockSpec((3, 1, rows, width), lambda i: (0, i, 0, 0)),
            half,
            half,
            fixed_out((8, width)),
        ],
        out_shape=[
            jax.ShapeDtypeStruct((near, rows, width), BF16),
            jax.ShapeDtypeStruct((3, near, rows, width), BF16),
            jax.ShapeDtypeStruct((near, quarter, width), F32),
            jax.ShapeDtypeStruct((near, quarter, width), BF16),
            jax.ShapeDtypeStruct((8, width), F32),
        ],
        compiler_params=params(40),
        cost_estimate=cost(2 * near * rows * width * 3 * width, 20e6),
        name="project_back",
    )(query, own, received, embedded, attn, mask, gain, shift, weight)


def swap(values, axis, bit):
    size = lax.axis_size(axis)
    return lax.ppermute(values, axis, [(place, place ^ bit) for place in range(size)])


def own_bit(axis, bit):
    return (lax.axis_index(axis) // bit) % 2


def pick(values, dim, which):
    return lax.dynamic_index_in_dim(values, which, dim, keepdims=False)


def add_in(kept, received):
    return (kept.astype(jnp.float32) + received.astype(jnp.float32)).astype(kept.dtype)


def halve(values, dim, axis, bit):
    mine = own_bit(axis, bit)
    received = swap(pick(values, dim, 1 - mine), axis, bit)
    return add_in(pick(values, dim, mine), received)


def join(values, dim, axis, bit):
    mine = own_bit(axis, bit)
    received = swap(values, axis, bit)
    first = jnp.where(mine == 0, values, received)
    second = jnp.where(mine == 0, received, values)
    return jnp.concatenate([first, second], axis=dim)


def reduce_rows(grad, order):
    dp = lax.axis_size("dp")
    rows, columns = grad.shape
    steps = dp.bit_length() - 1
    part = rows // dp
    if columns % 512 == 0:
        tail = (1, 2, part, 2, columns // 4, 2)
        parts = grad.reshape((2,) * steps + (part, 4, columns // 4))
        parts = jnp.moveaxis(parts, steps + 1, 0)
    else:
        parts = grad.reshape((2,) * steps + (4, part // 4, columns))
        parts = jnp.moveaxis(parts, steps, 0)
    parts = parts.reshape((2, 2) + parts.shape[1:])
    names = ["core", "y"] + [1 << bit for bit in reversed(range(steps))]
    for name in order(steps):
        dim = names.index(name)
        if name == "core":
            parts = halve(parts, dim, "seq", 1)
        elif name == "y":
            parts = halve(parts, dim, "seq", 2)
        else:
            parts = halve(parts, dim, "dp", name)
        names.pop(dim)
    parts = join(parts[None], 0, "seq", 2)
    parts = join(parts[None], 0, "seq", 1)
    parts = parts.reshape((4,) + parts.shape[2:]).astype(jnp.float32)
    if columns % 512 == 0:
        return jnp.moveaxis(parts, 0, 1).reshape(part, columns)
    return parts.reshape(part, columns)


def x_first(steps):
    return ["core"] + [1 << bit for bit in range(steps)] + ["y"]


def y_first(steps):
    return ["core", "y"] + [1 << bit for bit in range(steps)]


def z_first(steps):
    return ["core"] + [1 << bit for bit in range(1, steps)] + [1, "y"]


def reduce_vector(values):
    dp = lax.axis_size("dp")
    steps = dp.bit_length() - 1
    values = values + swap(values, "seq", 1)
    values = values + swap(values, "seq", 2)
    values = values.reshape((2,) * steps + values.shape[1:])
    for bit in reversed(range(steps)):
        mine = own_bit("dp", 1 << bit)
        received = swap(pick(values, 0, 1 - mine), "dp", 1 << bit)
        values = pick(values, 0, mine) + received
    return values


def any_places(
    patches,
    targets,
    mask_order,
    mask_count,
    attend_gain,
    attend_shift,
    joint_weight,
    query_bias,
    value_bias,
    output_weight,
    output_bias,
    feed_gain,
    feed_shift,
    expand_weight,
    expand_bias,
    reduce_weight,
    reduce_bias,
    pixel_weight,
    pixel_bias,
    mask_token,
):
    images, quarter, features = patches.shape
    dp = lax.axis_size("dp")
    near = images // 2
    rows_one = 2 * quarter
    row_count = near * rows_one
    place_y = own_bit("seq", 2)

    def own_and_far(values):
        parts = values.reshape((2, near) + values.shape[1:])
        return pick(parts, 0, place_y), swap(pick(parts, 0, 1 - place_y), "seq", 2)

    def line(vector):
        return vector.astype(F32)[None, :]

    masked_here = mask_order < mask_count[:, None]
    embedded_here = jnp.where(masked_here[:, :, None], mask_token[None, None, :], patches)
    embedded_own, embedded_far = own_and_far(embedded_here)
    mask = jnp.concatenate(own_and_far(masked_here.astype(jnp.int32)), axis=1)
    mask = mask.astype(F32)[:, :, None]
    count_sum = jnp.sum(mask_count)
    for bit in range(dp.bit_length() - 1):
        count_sum = count_sum + swap(count_sum, "dp", 1 << bit)
    inverse = 1.0 / (count_sum.astype(F32) * PIXELS)
    target_own, target_far = own_and_far(targets)
    joint_bias = jnp.concatenate(
        [line(query_bias), jnp.zeros((1, features), F32), line(value_bias)], axis=1
    )
    biases = jnp.concatenate(
        [
            line(vector)
            for vector in (output_bias, feed_gain, feed_shift, reduce_bias, pixel_bias)
        ]
        + [jnp.zeros((3, features), F32)],
        axis=0,
    )
    embedded, joint = project(
        embedded_own, embedded_far, line(attend_gain), line(attend_shift), joint_weight, joint_bias
    )
    pairs_far = swap(joint[:, 1:], "seq", 1)
    mixed, probs = attend(joint, pairs_far)
    (
        input_two,
        activated,
        after_low,
        grad_pred,
        grad_branch,
        grad_expand,
        grad_out,
        grad_attn,
        grad_mixed,
        sums_two,
    ) = rows_step(
        inverse.reshape(1, 1),
        embedded,
        mixed,
        mask,
        target_own,
        target_far,
        output_weight,
        expand_weight,
        reduce_weight,
        pixel_weight,
        biases,
        line(expand_bias),
    )

    def flat(values):
        return values.reshape(row_count, values.shape[-1])

    reduce_weight_grad = outer(flat(activated), flat(grad_branch))
    expand_weight_grad = outer(flat(input_two), flat(grad_expand))
    pixel_weight_grad = outer(flat(after_low), flat(grad_pred))
    output_weight_grad = outer(flat(mixed), flat(grad_out))
    square_grads = jnp.concatenate([pixel_weight_grad, output_weight_grad], axis=1)
    grad_query, grad_own, grad_far = attend_back(joint, pairs_far, probs, grad_mixed)
    received = swap(grad_far, "seq", 1)
    input_one, grad_joint, patch_near, patch_far, sums_one = project_back(
        grad_query,
        grad_own,
        received,
        embedded,
        grad_attn,
        mask,
        line(attend_gain),
        line(attend_shift),
        joint_weight,
    )
    grad_joint = grad_joint.reshape(3, row_count, features)
    joint_weight_grad = jnp.concatenate(
        [outer(flat(input_one), grad_joint[part]) for part in range(3)], axis=1
    )
    patch_far = swap(patch_far, "seq", 2).astype(F32)
    patch_grad = jnp.concatenate(
        [
            jnp.where(place_y == 0, patch_near, patch_far),
            jnp.where(place_y == 0, patch_far, patch_near),
        ],
        axis=0,
    )
    hidden = expand_bias.shape[0]
    vectors = (
        sums_one[0],
        sums_one[1],
        sums_one[2],
        sums_one[3],
        sums_two[4],
        sums_two[2],
        sums_two[3],
        sums_two[6 : 6 + hidden // features].reshape(hidden),
        sums_two[1],
        sums_two[0],
        sums_one[4],
    )
    loss_part = jnp.sum(sums_two[5]) * inverse
    lengths = [vector.shape[0] // dp for vector in vectors]
    packed = jnp.concatenate(
        [vector.reshape(dp, -1) for vector in vectors]
        + [jnp.broadcast_to(loss_part[None, None], (dp, 1))],
        axis=1,
    )
    packed = reduce_vector(packed)
    loss_value = packed[-1]
    cuts, start = [], 0
    for length in lengths:
        cuts.append(packed[start : start + length])
        start += length
    (
        attend_gain_grad,
        attend_shift_grad,
        query_bias_grad,
        value_bias_grad,
        output_bias_grad,
        feed_gain_grad,
        feed_shift_grad,
        expand_bias_grad,
        reduce_bias_grad,
        pixel_bias_grad,
        mask_token_grad,
    ) = cuts
    reduce_weight_grad = reduce_rows(reduce_weight_grad, x_first)
    expand_weight_grad = reduce_rows(expand_weight_grad, y_first)
    square_grads = reduce_rows(square_grads, z_first)
    joint_weight_grad = reduce_rows(joint_weight_grad, x_first)
    return (
        loss_value,
        attend_gain_grad,
        attend_shift_grad,
        joint_weight_grad,
        query_bias_grad,
        value_bias_grad,
        square_grads[:, PIXELS:],
        output_bias_grad,
        feed_gain_grad,
        feed_shift_grad,
        expand_weight_grad,
        expand_bias_grad,
        reduce_weight_grad,
        reduce_bias_grad,
        square_grads[:, :PIXELS],
        pixel_bias_grad,
        mask_token_grad,
        patch_grad,
    )


MESH = pl.DeviceIdType.MESH


def places():
    data, seq = lax.axis_index("dp"), lax.axis_index("seq")
    x, low, high = lax.rem(data, 2), lax.rem(lax.div(data, 2), 2), lax.div(data, 4)
    core, y = lax.rem(seq, 2), lax.div(seq, 2)
    return {
        "x": (x, {"dp": data + 1 - 2 * x}),
        "low": (low, {"dp": data + 2 - 4 * low}),
        "high": (high, {"dp": data + 4 - 8 * high}),
        "y": (y, {"seq": seq + 2 - 4 * y}),
        "core": (core, {"seq": seq + 1 - 2 * core}),
    }


def greet(where):
    barrier = pltpu.get_barrier_semaphore()
    for _, partner in where.values():
        pl.semaphore_signal(barrier, inc=1, device_id=partner, device_id_type=MESH)
    pl.semaphore_wait(barrier, len(where))


def remote(source, target, send, receive, partner):
    return pltpu.make_async_remote_copy(
        src_ref=source,
        dst_ref=target,
        send_sem=send,
        recv_sem=receive,
        device_id=partner,
        device_id_type=MESH,
    )


NAMES = ("high", "low", "x", "y")


def stage_shapes(names, order, tail):
    names, shapes = list(names), []
    for token in order:
        if token == "Gy":
            names = ["y"]
        elif token == "Gcore":
            names = ["core"] + names
        elif token[0] != "+":
            names.remove(token)
        shapes.append((2,) * len(names) + tail)
    return shapes


def for_each(dims, body):
    outer = max(dims - 2, 0)
    inner = list(itertools.product(range(2), repeat=dims - outer))
    if outer == 0:
        for spot in inner:
            body(spot)
        return

    def one(place, carry):
        first = tuple(lax.rem(lax.div(place, 2 ** (outer - 1 - dim)), 2) for dim in range(outer))
        for spot in inner:
            body(first + spot)
        return carry

    lax.fori_loop(0, 2**outer, one, 0)


def add_up(target, place, other):
    target[place] = (target[place].astype(F32) + other.astype(F32)).astype(target.dtype)


class Chain:
    def __init__(self, where, start, names, order, buffers, send, receive, base, swapped=None):
        self.where, self.order = dict(where), order
        if swapped is not None:
            (first, partner_first), (second, partner_second) = (where[name] for name in swapped)
            core = where["core"][0]

            def chosen(zero, one):
                return zero + core * (one - zero)

            for name, place, ours, other in (
                (swapped[0], (first, second), partner_first, partner_second),
                (swapped[1], (second, first), partner_second, partner_first),
            ):
                here = {"dp": lax.axis_index("dp"), "seq": lax.axis_index("seq")}
                ours, other = {**here, **ours}, {**here, **other}
                partner = {axis: chosen(ours[axis], other[axis]) for axis in here}
                self.where[name] = (chosen(*place), partner)
        self.plain = where
        self.refs = [start] + list(buffers)
        self.send, self.receive, self.base = send, receive, base
        self.names = [list(names)]
        for token in order:
            names = list(self.names[-1])
            if token == "Gy":
                names = ["y"]
            elif token == "Gcore":
                names = ["core"] + names
            elif token[0] != "+":
                names.remove(token)
            self.names.append(names)

    def copies(self, stage):
        token = self.order[stage]
        source, target = self.refs[stage], self.refs[stage + 1]
        if token[0] == "+":
            _, partner = self.plain[token[1:]]
        elif token[0] == "G":
            place, partner = self.plain[token[1:]]
            target = target.at[place]
        else:
            place, partner = self.where[token]
            dim = self.names[stage].index(token)
            source = source.at[(slice(None),) * dim + (1 - place,)]
        base = 2 * (self.base + stage)
        if len(source.shape) > 2:
            pairs = [(source.at[half], target.at[half]) for half in range(2)]
        else:
            pairs = [(source, target)]
        return [
            remote(one, other, self.send.at[base + index], self.receive.at[base + index], partner)
            for index, (one, other) in enumerate(pairs)
        ]

    def start(self, stage):
        for copy in self.copies(stage):
            copy.start()

    def finish(self, stage):
        for copy in self.copies(stage):
            copy.wait()
        token = self.order[stage]
        source, target = self.refs[stage], self.refs[stage + 1]
        if token[0] == "G":
            place, _ = self.plain[token[1:]]
            target[place] = source[...]
            return
        dim = None
        if token[0] != "+":
            place, _ = self.where[token]
            dim = self.names[stage].index(token)

        def one(spot):
            origin = spot if dim is None else spot[:dim] + (place,) + spot[dim:]
            add_up(target, spot if spot else Ellipsis, source[origin if origin else Ellipsis])

        for_each(len(self.names[stage + 1]), one)

    def turn(self, stage):
        if stage > 0:
            self.finish(stage - 1)
        if stage < len(self.order):
            self.start(stage)


Y_FIRST = ("y", "x", "low", "high", "Gy", "Gcore")
Y_THEN_LOW = ("y", "low", "x", "high", "Gy", "Gcore")
X_FIRST = ("x", "low", "high", "+y", "Gcore")
SUMS_ORDER = ("+core", "+y", "+x", "+low", "+high")
MOST = 6
TILE_ORDERS = (
    X_FIRST,
    Y_FIRST,
    Y_THEN_LOW,
    Y_THEN_LOW,
    Y_FIRST,
    Y_FIRST,
    Y_FIRST,
    X_FIRST,
    X_FIRST,
    Y_THEN_LOW,
    Y_FIRST,
    Y_FIRST,
    X_FIRST,
)
TILE_SWAPS = (
    ("x", "low"),
    ("x", "y"),
    ("y", "low"),
    ("y", "low"),
    ("x", "y"),
    ("x", "y"),
    ("x", "y"),
    ("x", "low"),
    ("x", "low"),
    ("y", "low"),
    ("x", "y"),
    ("x", "y"),
    ("x", "low"),
)
TILES = len(TILE_ORDERS)
TILE_STEPS = (0, 1, 2, 3, 4, 5, 6, 7, 8, 10, 18, 25, 31)
TURNS = {
    2: ((0, 0),),
    3: ((1, 0),),
    4: ((0, 1), (2, 0),),
    5: ((1, 1), (3, 0),),
    6: ((0, 2), (4, 0),),
    7: ((1, 2), (2, 1), (5, 0),),
    8: ((0, 3), (3, 1), (6, 0),),
    9: ((1, 3), (7, 0),),
    10: ((0, 4), (1, 4), (2, 2), (4, 1), (8, 0),),
    11: ((0, 5), (3, 2), (7, 1), (13, 0),),
    12: ((9, 0), (1, 5), (2, 3), (5, 1), (13, 1), (6, 1),),
    14: ((1, 6), (3, 3),),
    15: ((2, 4), (4, 2),),
    16: ((7, 2), (13, 2),),
    17: ((3, 4),),
    18: ((2, 5), (4, 3), (5, 2),),
    19: ((2, 6), (3, 5), (7, 3), (13, 3), (6, 2), (8, 1), (9, 1),),
    20: ((4, 4), (5, 3), (10, 0), (3, 6),),
    21: ((7, 4), (13, 4),),
    22: ((4, 5), (5, 4),),
    23: ((7, 5), (6, 3),),
    24: ((4, 6), (13, 5),),
    25: ((5, 5), (8, 2), (9, 2), (10, 1),),
    26: ((5, 6), (6, 4),),
    27: ((9, 3), (11, 0), (6, 5), (8, 3), (10, 2),),
    28: ((9, 4),),
    29: ((6, 6),),
    30: ((10, 3),),
    31: ((9, 5), (8, 4),),
    32: ((9, 6), (8, 5), (10, 4), (11, 1),),
    33: ((12, 0), (10, 5),),
}
LAST_TURNS = (
    (14, 0),
    (10, 6),
    (14, 1),
    (11, 2),
    (12, 1),
    (11, 3),
    (14, 2),
    (12, 2),
    (14, 3),
    (11, 4),
    (14, 4),
    (12, 3),
    (11, 5),
    (14, 5),
    (11, 6),
    (12, 4),
    (12, 5),
)


def chain_scratch(cases):
    scratch, counts = [], []
    for names, order, tail, dtype in cases:
        shapes = stage_shapes(names, order, tail)
        scratch += [pltpu.VMEM(shape, dtype) for shape in shapes]
        counts.append(len(shapes))
    return scratch, counts


def split_list(values, counts):
    parts, start = [], 0
    for count in counts:
        parts.append(values[start : start + count])
        start += count
    return parts


GAIN_ONE, SHIFT_ONE, QUERY, VALUE, OUTPUT, GAIN_TWO, SHIFT_TWO, REDUCE, PIXEL, TOKEN, EXPAND = range(11)
FRONT_OWN = 6
FRONT_FAR = 9
FRONT_ATTEND = 12


def lines_kernel(*refs):
    out = refs[-1]
    row = 0
    for ref in refs[:-1]:
        for start in range(0, ref.shape[0], WIDE):
            out[row : row + 1] = ref[start : start + WIDE].astype(F32).reshape(1, WIDE)
            row += 1


def stack_lines(*vectors):
    return pl.pallas_call(
        lines_kernel,
        in_specs=[pl.BlockSpec(memory_space=pltpu.VMEM)] * len(vectors),
        out_specs=pl.BlockSpec(memory_space=pltpu.VMEM),
        out_shape=jax.ShapeDtypeStruct((16, WIDE), F32),
        cost_estimate=cost(1e4, 1e5),
        name="stack_lines",
    )(*vectors)


def column_of(line):
    count = line.shape[1]
    down = lax.broadcasted_iota(jnp.int32, (count, count), 0)
    along = lax.broadcasted_iota(jnp.int32, (count, count), 1)
    return jnp.sum(jnp.where(down == along, jnp.broadcast_to(line, (count, count)), 0.0), axis=1, keepdims=True)


def front_kernel(
    parts, counts, rows_in, targets_in, orders_in, lines, weight_in, pixel_in, expand_in, output_in,
    embedded_out, input_out, joint_out, pairs_out, mixed_out, probs_out, masks_out, target_out, expand_out,
    embedded, inputs, masks, order_far, joint, pairs, weight, pixel, expand, output,
    local, far_send, far_receive, send, receive,
):
    images, heads = joint.shape[:2]
    quarter = rows_in.shape[2]
    where = {name: places()[name] for name in ("core", "y")}
    sibling = where["core"][1]
    y, other = where["y"]
    step = pl.program_id(0)
    near_half, far_half = pl.ds(0, quarter), pl.ds(quarter, quarter)

    def pair_copy(image):
        return remote(
            joint.at[image, :, pl.ds(1, 2)], pairs.at[image], send.at[image], receive.at[image], sibling
        )

    def far_copy(index, source, target):
        return remote(source, target, far_send.at[index], far_receive.at[index], other)

    order_copy = far_copy(0, orders_in.at[1 - y], order_far)
    row_copies = [
        far_copy(1 + image, rows_in.at[1 - y, image], embedded.at[image, far_half]) for image in range(images)
    ]
    target_copies = [
        far_copy(1 + images + image, targets_in.at[1 - y, image], target_out.at[image, far_half])
        for image in range(images)
    ]
    own_copy = pltpu.make_async_copy(rows_in.at[y], embedded.at[:, near_half], local.at[0])
    target_copy = pltpu.make_async_copy(targets_in.at[y], target_out.at[:, near_half], local.at[1])
    loads = [
        pltpu.make_async_copy(source, target, local.at[2 + index])
        for index, (source, target) in enumerate(
            ((pixel_in, pixel), (expand_in, expand), (output_in, output), (weight_in, weight))
        )
    ]

    @pl.when(step == 0)
    def _():
        own_copy.start()
        greet(where)
        order_copy.start()
        for copy in row_copies + loads:
            copy.start()
        target_copy.start()
        loads[0].wait()
        expand_out[0] = pixel[...]

    @pl.when(step == parts + 1)
    def _():
        loads[2].wait()
        expand_out[0] = output[...]

    for part in range(parts):

        @pl.when(step == 1 + part)
        def _(part=part):
            if part == 0:
                loads[1].wait()
            span = weight.shape[0] // 8
            starts = [place * parts * span + part * span for place in range(8)]
            expand_out[0] = jnp.concatenate([expand[:, start : start + span] for start in starts], axis=1)

    def project(image, start, order):
        block = pl.ds(start, quarter)
        mask = column_of((order < counts[y * images + image]).astype(F32))
        masks[image, block] = mask
        token = lines[TOKEN : TOKEN + 1].astype(BF16)
        rows = jnp.where(mask > 0.5, token, embedded[image, block])
        embedded[image, block] = rows
        normed, _ = normalize(rows.astype(F32))
        gain, shift = lines[GAIN_ONE : GAIN_ONE + 1], lines[SHIFT_ONE : SHIFT_ONE + 1]
        low = (normed * gain + shift).astype(BF16)
        inputs[image, block] = low
        for part, bias in ((1, None), (2, lines[VALUE : VALUE + 1]), (0, lines[QUERY : QUERY + 1])):
            total = dot(low, weight[:, part * WIDE : (part + 1) * WIDE])
            total = (total if bias is None else total + bias).astype(BF16)
            for pair in range(heads):
                joint[image, pair, part, block] = total[:, pair * PAIR : (pair + 1) * PAIR]

    @pl.when((step >= FRONT_OWN) & (step < FRONT_FAR))
    def _():
        @pl.when(step == FRONT_OWN)
        def _():
            own_copy.wait()
            loads[3].wait()

        image = step - FRONT_OWN
        project(image, 0, orders_in[y, image, 0:1, :quarter])

    @pl.when((step >= FRONT_FAR) & (step < FRONT_ATTEND))
    def _():
        for index in range(images):

            @pl.when(step == FRONT_FAR + index)
            def _(index=index):
                if index == 0:
                    order_copy.wait()
                row_copies[index].wait()
                target_copies[index].start()

        image = step - FRONT_FAR
        project(image, quarter, order_far[image, 0:1, :quarter])
        pair_copy(image).start()
        embedded_out[0] = embedded[image]
        input_out[0] = inputs[image]
        joint_out[0] = joint[image]
        masks_out[0] = masks[image]

    @pl.when(step >= FRONT_ATTEND)
    def _():
        place = step - FRONT_ATTEND
        image, pair = lax.div(place, heads), lax.rem(place, heads)

        @pl.when(pair == 0)
        def _():
            pair_copy(image).wait()

        queries = side_by_side(joint[image, pair, 0] * jnp.asarray(HEAD_DIM**-0.5, BF16))
        keys_in = jnp.concatenate([joint[image, pair, 1], pairs[image, pair, 0]], axis=0)
        values_in = jnp.concatenate([joint[image, pair, 2], pairs[image, pair, 1]], axis=0)
        pairs_out[0, 0] = pairs[image, pair]
        scores = dot_nt(keys_in, queries)
        exponent = jnp.exp(scores - jnp.max(scores, axis=0, keepdims=True))
        total = jnp.sum(exponent, axis=0, keepdims=True)
        probs = (exponent * (1.0 / total)).astype(BF16)
        probs_out[0, 0] = probs
        mixed_out[0] = merge_turned(dot_tn(values_in, probs)).astype(BF16)

    @pl.when(step == pl.num_programs(0) - 1)
    def _():
        for copy in target_copies:
            copy.wait()
        target_copy.wait()


def merge_turned(stacked):
    rows = stacked.shape[1] // 2
    down = lax.broadcasted_iota(jnp.int32, (PAIR, rows), 0)
    return jnp.where(down < HEAD_DIM, stacked[:, :rows], stacked[:, rows:]).T


def front(counts, rows_in, targets_in, orders_in, lines, weight, pixel, expand, output):
    near, quarter, width = rows_in.shape[1:]
    rows, heads = 2 * quarter, width // PAIR
    parts = expand.shape[1] // width

    def image(step):
        return jnp.clip(step - FRONT_FAR, 0, near - 1)

    def spot(step):
        place = jnp.maximum(step - FRONT_ATTEND, 0)
        return lax.div(place, heads), lax.rem(place, heads)

    block = pl.BlockSpec((1, rows, width), lambda s: (image(s), 0, 0))
    return pl.pallas_call(
        partial(front_kernel, parts),
        grid=(FRONT_ATTEND + near * heads,),
        in_specs=[
            pl.BlockSpec(memory_space=pltpu.SMEM),
            pl.BlockSpec(memory_space=pl.ANY),
            pl.BlockSpec(memory_space=pl.ANY),
            fixed(orders_in.shape),
            fixed(lines.shape),
        ]
        + [pl.BlockSpec(memory_space=pl.ANY)] * 4,
        out_specs=[
            block,
            block,
            pl.BlockSpec((1, heads, 3, rows, PAIR), lambda s: (image(s), 0, 0, 0, 0)),
            pl.BlockSpec((1, 1, 2, rows, PAIR), lambda s: spot(s) + (0, 0, 0)),
            pl.BlockSpec((1, rows, PAIR), lambda s: (spot(s)[0], 0, spot(s)[1])),
            pl.BlockSpec((1, 1, 2 * rows, 2 * rows), lambda s: spot(s) + (0, 0)),
            pl.BlockSpec((1, rows, 1), lambda s: (image(s), 0, 0)),
            pl.BlockSpec(memory_space=pl.ANY),
            pl.BlockSpec((1, width, width), lambda s: (jnp.minimum(s, parts + 1), 0, 0)),
        ],
        out_shape=[
            jax.ShapeDtypeStruct((near, rows, width), BF16),
            jax.ShapeDtypeStruct((near, rows, width), BF16),
            jax.ShapeDtypeStruct((near, heads, 3, rows, PAIR), BF16),
            jax.ShapeDtypeStruct((near, heads, 2, rows, PAIR), BF16),
            jax.ShapeDtypeStruct((near, rows, width), BF16),
            jax.ShapeDtypeStruct((near, heads, 2 * rows, 2 * rows), BF16),
            jax.ShapeDtypeStruct((near, rows, 1), F32),
            jax.ShapeDtypeStruct((near, rows, width), BF16),
            jax.ShapeDtypeStruct((parts + 2, width, width), BF16),
        ],
        scratch_shapes=[
            pltpu.VMEM((near, rows, width), BF16),
            pltpu.VMEM((near, rows, width), BF16),
            pltpu.VMEM((near, rows, 1), F32),
            pltpu.VMEM(orders_in.shape[1:], jnp.int32),
            pltpu.VMEM((near, heads, 3, rows, PAIR), BF16),
            pltpu.VMEM((near, heads, 2, rows, PAIR), BF16),
            pltpu.VMEM(weight.shape, BF16),
            pltpu.VMEM(pixel.shape, BF16),
            pltpu.VMEM(expand.shape, BF16),
            pltpu.VMEM(output.shape, BF16),
            pltpu.SemaphoreType.DMA((6,)),
            pltpu.SemaphoreType.DMA((1 + 2 * near,)),
            pltpu.SemaphoreType.DMA((1 + 2 * near,)),
            pltpu.SemaphoreType.DMA((near,)),
            pltpu.SemaphoreType.DMA((near,)),
        ],
        compiler_params=pltpu.CompilerParams(
            vmem_limit_bytes=60 * MIB, collective_id=1, has_side_effects=True
        ),
        cost_estimate=cost(5e9, 40e6),
        name="front",
    )(counts, rows_in, targets_in, orders_in, lines, weight, pixel, expand, output)


def middle_kernel(
    embedded_in, mixed, mask_in, target_in, weights, reduce, lines,
    lefts, rights, input_out, scaling_out, sums_out, low, total, biases,
):
    parts = reduce.shape[1]
    span = reduce.shape[2]
    width = weights.shape[1]
    mask = mask_in[0]

    @pl.when(pl.program_id(0) == 0)
    def _():
        sums_out[...] = jnp.zeros_like(sums_out)
        for part in range(parts):
            pieces = []
            for place in range(8):
                row, start = divmod((place * parts + part) * span, width)
                pieces.append(lines[EXPAND + row : EXPAND + row + 1, start : start + span])
            biases[part] = jnp.concatenate(pieces, axis=1)

    after_attn = embedded_in[0].astype(F32) + dot(mixed[0], weights[parts + 1]) + lines[OUTPUT : OUTPUT + 1]
    lefts[0, parts + 1] = mixed[0]
    normed, scaling = normalize(after_attn)
    rights[0, parts + 1] = normed.astype(BF16)
    scaling_out[0] = scaling
    low[...] = (normed * lines[GAIN_TWO : GAIN_TWO + 1] + lines[SHIFT_TWO : SHIFT_TWO + 1]).astype(BF16)
    input_out[0] = low[...]
    total[...] = after_attn + lines[REDUCE : REDUCE + 1]

    def one(part, carry):
        active, rate = gelu_both(dot(low[...], weights[1 + part]) + biases[part])
        active = active.astype(BF16)
        lefts[0, 1 + part] = active
        rights[0, 1 + part] = rate.astype(BF16)
        total[...] += dot(active, reduce[:, part].reshape(width, width))
        return carry

    for part in range(parts):
        one(part, 0)
    after_low = total[...].astype(BF16)
    lefts[0, 0] = after_low
    errors = dot(after_low, weights[0]) + lines[PIXEL : PIXEL + 1] - target_in[0].astype(F32)
    square = errors * errors + 1.0
    root = lax.rsqrt(square)
    grad_pred = (mask * errors * root).astype(BF16)
    rights[0, 0] = grad_pred
    sums_out[0:1] += column_sums(grad_pred)
    sums_out[5:6] += jnp.sum((square * root - 1.0) * mask, axis=0, keepdims=True)
    sums_out[10:11] += jnp.sum(jnp.broadcast_to(mask, errors.shape), axis=0, keepdims=True)


def middle(embedded, mixed, mask, targets, weights, reduce, lines):
    near, rows, width = embedded.shape
    parts = reduce.shape[1]
    block = pl.BlockSpec((1, rows, width), lambda i: (i, 0, 0))
    column = pl.BlockSpec((1, rows, 1), lambda i: (i, 0, 0))
    stack = pl.BlockSpec((1, parts + 2, rows, width), lambda i: (i, 0, 0, 0))
    return pl.pallas_call(
        middle_kernel,
        grid=(near,),
        in_specs=[
            block,
            block,
            column,
            block,
            fixed((parts + 2, width, width)),
            fixed(reduce.shape),
            fixed(lines.shape),
        ],
        out_specs=[stack, stack, block, column, fixed_out((16, width))],
        out_shape=[
            jax.ShapeDtypeStruct((near, parts + 2, rows, width), BF16),
            jax.ShapeDtypeStruct((near, parts + 2, rows, width), BF16),
            jax.ShapeDtypeStruct((near, rows, width), BF16),
            jax.ShapeDtypeStruct((near, rows, 1), F32),
            jax.ShapeDtypeStruct((16, width), F32),
        ],
        scratch_shapes=[
            pltpu.VMEM((rows, width), BF16),
            pltpu.VMEM((rows, width), F32),
            pltpu.VMEM((parts, 1, width), F32),
        ],
        compiler_params=params(60),
        cost_estimate=cost(2 * near * rows * width * width * (2 * parts + 2), 40e6),
        name="middle",
    )(embedded, mixed, mask, targets, weights, reduce, lines)


HIGH_ROWS = 4 * 96


def spread_half(result, target, high, start, swapped):
    for low in range(2):
        for x in range(2):
            for y in range(2):
                at = (low * 2 + x) * 96 + start
                piece = result[at : at + HALF, y * 384 : (y + 1) * 384]
                spot = {"high": high, "low": low, "x": x, "y": y}
                if swapped is not None:
                    first, second = swapped
                    spot[first], spot[second] = spot[second], spot[first]
                target[tuple(spot[name] for name in NAMES)] = piece.astype(BF16)


HALF = 48
SLOTS = 4
KEPT = 10
FIRST_ATTEND = 11
GROUP_STEPS = (18, 25, 31)
FIRST_NORM = 32


def back_kernel(
    counts, left, right, weights, reduce, query, key, value, input_two, scaling_two, input_one, joint, pairs, probs_in, lines, sums_in,
    embedded_in, mask_in, *rest,
):
    (
        done_out,
        near_out,
        far_out,
        sums_out,
        late_out,
        branch,
        wide,
        grad_in,
        upstream,
        own_pairs,
        give_pairs,
        got_pairs,
        far_give,
        sums,
        late,
        keep,
        give,
        got,
        send,
        receive,
        core_send,
        core_receive,
        pair_send,
        pair_receive,
        far_send,
        far_receive,
    ) = rest[:26]
    buffers = split_list(rest[26:], counts)
    where = places()
    core, sibling = where["core"]
    step = pl.program_id(0)
    images, rows, width = input_two.shape
    every = images * rows
    quarter = rows // 2
    heads = width // PAIR
    first_gain, second_gain = lines[GAIN_ONE : GAIN_ONE + 1], lines[GAIN_TWO : GAIN_TWO + 1]
    chains = [
        Chain(where, keep.at[unit % KEPT], NAMES, order, buffers[unit], send, receive, MOST * unit, TILE_SWAPS[unit])
        for unit, order in enumerate(TILE_ORDERS)
    ]
    chains.append(Chain(where, sums, (), SUMS_ORDER, buffers[TILES], send, receive, MOST * TILES))
    chains.append(Chain(where, late, (), SUMS_ORDER, buffers[TILES + 1], send, receive, MOST * TILES + MOST))

    def core_copy(unit):
        slot = lax.rem(unit, SLOTS)
        return remote(give.at[slot], got.at[slot], core_send.at[unit], core_receive.at[unit], sibling)

    def pair_copy(place):
        slot = lax.rem(place, SLOTS)
        return remote(
            give_pairs.at[slot], got_pairs.at[place], pair_send.at[place], pair_receive.at[place], sibling
        )

    def far_copy(image):
        return remote(
            far_give.at[image], far_out.at[image], far_send.at[image], far_receive.at[image], where["y"][1]
        )

    def core_sum(unit):
        core_copy(unit).wait()
        for_each(4, lambda spot: add_up(keep.at[unit % KEPT], spot, got[(unit % SLOTS,) + spot]))

    def turn(unit, stage):
        if unit < TILES and stage == 0:
            core_sum(unit)
        chains[unit].turn(stage)
        if stage == len(chains[unit].order) and unit < TILES:
            done_out[unit] = chains[unit].refs[-1][...]

    def tile(unit, lines_of, value, swaps):
        def one(high, carry):
            columns = pl.ds(pl.multiple_of(high * HIGH_ROWS, HIGH_ROWS), HIGH_ROWS)
            result = dot_tn(lines_of(columns).reshape(every, HIGH_ROWS), value)
            for half in range(2):
                for swapped, chosen in [(None, True)] if half == 0 else swaps:

                    @pl.when(jnp.logical_and(core == half, chosen))
                    def _(half=half, swapped=swapped):
                        spread_half(result, keep.at[lax.rem(unit, KEPT)], high, half * HALF, swapped)

                    @pl.when(jnp.logical_and(core != half, chosen))
                    def _(half=half, swapped=swapped):
                        spread_half(result, give.at[lax.rem(unit, SLOTS)], high, half * HALF, swapped)

            return carry

        lax.fori_loop(0, 2, one, 0)
        core_copy(unit).start()

    def swaps_of(units, unit):
        kinds = []
        for other in units:
            if TILE_SWAPS[other] not in kinds:
                kinds.append(TILE_SWAPS[other])
        if len(kinds) == 1:
            return [(kinds[0], True)]
        found = []
        for kind in kinds:
            chosen = functools.reduce(
                jnp.logical_or, [unit == other for other in units if TILE_SWAPS[other] == kind]
            )
            found.append((kind, chosen))
        return found

    def flat(ref):
        return ref[...].reshape(every, ref.shape[-1])

    def left_lines(columns):
        return left[:, 0, :, columns]

    @pl.when(step == 0)
    def _():
        greet(where)
        sums[...] = sums_in[...]
        late[...] = jnp.zeros_like(late)
        grad_in[...] = jnp.zeros_like(grad_in)

    for at, turns in TURNS.items():

        @pl.when(step == at)
        def _(turns=turns):
            for unit, stage in turns:
                turn(unit, stage)

    @pl.when(step == 0)
    def _():
        tile(0, left_lines, right[:, 0].reshape(every, width), swaps_of((0,), 0))

        def one(image, carry):
            low = dot_nt(right[image, 0], weights[0]).astype(BF16)
            branch[image] = low
            sums[1:2] += column_sums(low)
            return carry

        lax.fori_loop(0, images, one, 0)

    @pl.when((step > 0) & (step < 9) & (lax.rem(step, 2) == 1))
    def _():
        tile(step, left_lines, flat(branch), swaps_of((1, 3, 5, 7), step))
        row = pl.ds(6 + lax.div(step, 2), 1)

        def one(image, carry):
            low = dot_nt(branch[image], reduce[:, 0].reshape(width, width)) * right[image, 0].astype(F32)
            low = low.astype(BF16)
            wide[image] = low
            sums[row] += column_sums(low)
            return carry

        lax.fori_loop(0, images, one, 0)

    @pl.when((step > 0) & (step < 9) & (lax.rem(step, 2) == 0))
    def _():
        tile(step, lambda columns: input_two[:, :, columns], flat(wide), swaps_of((2, 4, 6, 8), step))
        fresh = jnp.where(step == 2, 0.0, 1.0)

        def one(image, carry):
            grad_in[image] = grad_in[image] * fresh + dot_nt(wide[image], weights[0])
            return carry

        lax.fori_loop(0, images, one, 0)

    @pl.when(step == 9)
    def _():
        def one(image, carry):
            normed = right[image, 0].astype(F32)
            grad = grad_in[image]
            low = branch[image].astype(F32) + normalize_back(grad, normed, scaling_two[image], second_gain)
            low = low.astype(BF16)
            branch[image] = low
            sums[2:3] += column_sums(grad * normed)
            sums[3:4] += column_sums(grad)
            sums[4:5] += column_sums(low)
            mixed = dot_nt(low, weights[0]).astype(BF16)
            for pair in range(heads):
                upstream[image, pair] = mixed[:, pair * PAIR : (pair + 1) * PAIR]
            return carry

        lax.fori_loop(0, images, one, 0)

    @pl.when(step == 10)
    def _():
        tile(9, left_lines, flat(branch), swaps_of((9,), 9))

    attends = (step >= FIRST_ATTEND) & (step < GROUP_STEPS[2]) & (step != GROUP_STEPS[0]) & (step != GROUP_STEPS[1])

    @pl.when(attends)
    def _():
        place = attend_place(step)
        group, inside = lax.div(place, 6), lax.rem(place, 6)
        image, pair = lax.rem(inside, 3), group * 2 + lax.div(inside, 3)

        @pl.when(place >= SLOTS)
        def _():
            pair_copy(place - SLOTS).wait_send()

        scale = HEAD_DIM**-0.5
        target = own_pairs.at[lax.rem(group, 2), inside]
        away = give_pairs.at[lax.rem(place, SLOTS)]
        queries = side_by_side(joint[0, 0, 0])
        keys_in = jnp.concatenate([joint[0, 0, 1], pairs[0, 0, 0]], axis=0)
        values_in = jnp.concatenate([joint[0, 0, 2], pairs[0, 0, 1]], axis=0)
        grad_mixed = side_by_side(upstream[image, pair])
        probs = probs_in[0, 0]
        grad_probs = dot_nt(values_in, grad_mixed)
        broad = probs.astype(F32)
        weighted = broad * grad_probs
        inner = jnp.sum(weighted, axis=0, keepdims=True)
        grad_scores = (weighted - broad * inner).astype(BF16)
        grad_values = dot(probs, grad_mixed).astype(BF16)
        grad_keys = (dot(grad_scores, queries) * scale).astype(BF16)
        target[0] = (merge_turned(dot_tn(keys_in, grad_scores)) * scale).astype(BF16)
        target[1] = grad_keys[:rows]
        target[2] = grad_values[:rows]
        away[0] = grad_keys[rows:]
        away[1] = grad_values[rows:]
        pair_copy(place).start()

    @pl.when((step == GROUP_STEPS[0]) | (step == GROUP_STEPS[1]) | (step == GROUP_STEPS[2]))
    def _():
        group = jnp.where(step == GROUP_STEPS[0], 0, jnp.where(step == GROUP_STEPS[1], 1, 2))
        slot = lax.rem(group, 2)
        for inside in range(6):
            pair_copy(group * 6 + inside).wait_recv()
            image, second = inside % 3, inside // 3
            for part in range(3):
                piece = own_pairs[slot, inside, part]
                if part > 0:
                    piece = piece.astype(F32) + got_pairs[group * 6 + inside, part - 1].astype(F32)
                start = part * 2 * PAIR + second * PAIR
                wide[image, :, start : start + PAIR] = piece.astype(BF16)
        tile(10 + group, lambda columns: input_one[:, :, columns], flat(wide), swaps_of((10, 11, 12), 10 + group))
        columns = jnp.concatenate([query[...], key[...], value[...]], axis=1)
        fresh = jnp.where(group == 0, 0.0, 1.0)
        row = pl.ds(5 + group, 1)

        def one(image, carry):
            late[row] += column_sums(wide[image])
            grad_in[image] = grad_in[image] * fresh + dot_nt(wide[image], columns)
            return carry

        lax.fori_loop(0, images, one, 0)

    @pl.when(step >= FIRST_NORM)
    def _():
        image = step - FIRST_NORM
        mask = mask_in[0]
        normed, scaling = normalize(embedded_in[0].astype(F32))
        grad = grad_in[image]
        total = branch[image].astype(F32) + normalize_back(grad, normed, scaling, first_gain)
        kept = total * (1.0 - mask)
        near_out[0] = kept[:quarter]
        far_give[image] = kept[quarter:].astype(BF16)
        far_copy(image).start()
        late[0:1] += column_sums(grad * normed)
        late[1:2] += column_sums(grad)
        late[2:3] += column_sums(total * mask)

    @pl.when(step == pl.num_programs(0) - 1)
    def _():
        for unit, stage in LAST_TURNS:
            turn(unit, stage)
        for image in range(images):
            far_copy(image).wait()
        for place in range(3 * heads - SLOTS, 3 * heads):
            pair_copy(place).wait_send()
        sums_out[...] = chains[TILES].refs[-1][...]
        late_out[...] = chains[TILES + 1].refs[-1][...]


def attend_place(step):
    place = step - FIRST_ATTEND
    for at in GROUP_STEPS[:2]:
        place = place - jnp.where(step > at, 1, 0)
    return jnp.clip(place, 0, 17)


def back(
    lefts, rights, weights, reduce, joint_weight, input_two, scaling_two, input_one, joint, pairs, probs, lines, sums, embedded, mask
):
    near, slots, rows, width = lefts.shape
    quarter = rows // 2
    heads = width // PAIR

    def slot(step):
        return jnp.minimum(lax.div(step + 1, 2), slots - 1)

    def part(step):
        return jnp.clip(lax.div(step - 1, 2), 0, slots - 3)

    def group(step):
        return jnp.where(step > GROUP_STEPS[0], 1, 0) + jnp.where(step > GROUP_STEPS[1], 1, 0)

    def columns(which):
        return pl.BlockSpec((width, 2 * PAIR), lambda s: (0, which * 3 + group(s)))

    def spot(step):
        place = attend_place(step)
        group, inside = lax.div(place, 6), lax.rem(place, 6)
        return lax.rem(inside, 3), group * 2 + lax.div(inside, 3)

    def image(step):
        return jnp.maximum(step - FIRST_NORM, 0)

    cases = [(NAMES, order, (HALF, 384), BF16) for order in TILE_ORDERS]
    cases.append(((), SUMS_ORDER, sums.shape, F32))
    cases.append(((), SUMS_ORDER, (8, width), F32))
    buffers, counts = chain_scratch(cases)
    whole = (2, 2, 2, 2, HALF, 384)
    stack = pl.BlockSpec((near, 1, rows, width), lambda s: (0, slot(s), 0, 0))
    return pl.pallas_call(
        partial(back_kernel, counts),
        grid=(FIRST_NORM + near,),
        in_specs=[
            stack,
            stack,
            pl.BlockSpec((1, width, width), lambda s: (slot(s), 0, 0)),
            pl.BlockSpec((8, 1, reduce.shape[2], width), lambda s: (0, part(s), 0, 0)),
            columns(0),
            columns(1),
            columns(2),
            fixed((near, rows, width)),
            fixed((near, rows, 1)),
            fixed((near, rows, width)),
            pl.BlockSpec((1, 1, 3, rows, PAIR), lambda s: spot(s) + (0, 0, 0)),
            pl.BlockSpec((1, 1, 2, rows, PAIR), lambda s: spot(s) + (0, 0, 0)),
            pl.BlockSpec((1, 1, 2 * rows, 2 * rows), lambda s: spot(s) + (0, 0)),
            fixed(lines.shape),
            fixed(sums.shape),
            pl.BlockSpec((1, rows, width), lambda s: (image(s), 0, 0)),
            pl.BlockSpec((1, rows, 1), lambda s: (image(s), 0, 0)),
        ],
        out_specs=[
            fixed((TILES, 2, 2, HALF, 384)),
            pl.BlockSpec((1, quarter, width), lambda s: (image(s), 0, 0)),
            pl.BlockSpec(memory_space=pl.ANY),
            fixed_out(sums.shape),
            fixed_out((8, width)),
        ],
        out_shape=[
            jax.ShapeDtypeStruct((TILES, 2, 2, HALF, 384), BF16),
            jax.ShapeDtypeStruct((near, quarter, width), F32),
            jax.ShapeDtypeStruct((near, quarter, width), BF16),
            jax.ShapeDtypeStruct(sums.shape, F32),
            jax.ShapeDtypeStruct((8, width), F32),
        ],
        scratch_shapes=[
            pltpu.VMEM((near, rows, width), BF16),
            pltpu.VMEM((near, rows, width), BF16),
            pltpu.VMEM((near, rows, width), F32),
            pltpu.VMEM((near, heads, rows, PAIR), BF16),
            pltpu.VMEM((2, 6, 3, rows, PAIR), BF16),
            pltpu.VMEM((SLOTS, 2, rows, PAIR), BF16),
            pltpu.VMEM((near * heads, 2, rows, PAIR), BF16),
            pltpu.VMEM((near, quarter, width), BF16),
            pltpu.VMEM(sums.shape, F32),
            pltpu.VMEM((8, width), F32),
            pltpu.VMEM((KEPT,) + whole, BF16),
            pltpu.VMEM((SLOTS,) + whole, BF16),
            pltpu.VMEM((SLOTS,) + whole, BF16),
            pltpu.SemaphoreType.DMA((2 * MOST * (TILES + 2),)),
            pltpu.SemaphoreType.DMA((2 * MOST * (TILES + 2),)),
            pltpu.SemaphoreType.DMA((TILES,)),
            pltpu.SemaphoreType.DMA((TILES,)),
            pltpu.SemaphoreType.DMA((near * heads,)),
            pltpu.SemaphoreType.DMA((near * heads,)),
            pltpu.SemaphoreType.DMA((near,)),
            pltpu.SemaphoreType.DMA((near,)),
        ]
        + buffers,
        compiler_params=pltpu.CompilerParams(
            vmem_limit_bytes=60 * MIB, collective_id=2, has_side_effects=True
        ),
        cost_estimate=cost(40e9, 60e6),
        name="back",
    )(
        lefts, rights, weights, reduce, joint_weight, joint_weight, joint_weight, input_two,
        scaling_two, input_one, joint, pairs, probs, lines, sums, embedded, mask,
    )


def emit_kernel(parts, place, done, near_in, far_in, sums, late, *outs):
    (
        loss, attend_gain, attend_shift, joint, query_bias, value_bias, output, output_bias, feed_gain,
        feed_shift, expand, expand_bias, reduce, reduce_bias, pixel, pixel_bias, token, patch,
    ) = outs
    data, y = place[0], place[1]
    inverse = 1.0 / (sums[10:11] * PIXELS)
    loss[...] = jnp.sum(sums[5:6] * inverse, axis=1, keepdims=True)
    wide_inverse = inverse[:, :384]

    def piece(unit, core, half):
        return done[unit, core, half].astype(F32) * wide_inverse

    def square(unit):
        return [
            jnp.concatenate([piece(unit, core, half) for half in range(2)], axis=1) for core in range(2)
        ]

    for unit, target in ((0, pixel), (2 * parts + 1, output)):
        for core, lines in enumerate(square(unit)):
            target[core * HALF : (core + 1) * HALF] = lines
    expands = []
    for part in range(parts):
        for core, lines in enumerate(square(1 + 2 * part)):
            start = part * 2 * HALF + core * HALF
            reduce[start : start + HALF] = lines
        expands.append(square(2 + 2 * part))
    span = 2 * HALF
    for core in range(2):
        for d in range(8):
            lines = [expands[part][core][:, d * span : (d + 1) * span] for part in range(parts)]
            expand[core * HALF : (core + 1) * HALF, d * 4 * span : (d + 1) * 4 * span] = jnp.concatenate(
                lines, axis=1
            )
    for group in range(3):
        for core, lines in enumerate(square(2 * parts + 2 + group)):
            for part in range(3):
                start = part * WIDE + group * 2 * PAIR
                joint[core * HALF : (core + 1) * HALF, start : start + 2 * PAIR] = lines[
                    :, part * 2 * PAIR : (part + 1) * 2 * PAIR
                ]

    def own_cut(lines):
        shift = lax.rem(WIDE - data * span, WIDE)
        return pltpu.roll(lines, shift, axis=1)[:, :span]

    early = own_cut(sums[...] * inverse)
    later = own_cut(late[...] * inverse)
    queries = jnp.concatenate([late[5 + group : 6 + group, : 2 * PAIR] for group in range(3)], axis=1)
    values = jnp.concatenate([late[5 + group : 6 + group, 4 * PAIR :] for group in range(3)], axis=1)
    both = jnp.concatenate([queries, values] + [jnp.zeros((6, WIDE), F32)], axis=0)
    both = own_cut(both * inverse)
    for target, lines, row in (
        (attend_gain, later, 0),
        (attend_shift, later, 1),
        (query_bias, both, 0),
        (value_bias, both, 1),
        (output_bias, early, 4),
        (feed_gain, early, 2),
        (feed_shift, early, 3),
        (reduce_bias, early, 1),
        (pixel_bias, early, 0),
        (token, later, 2),
    ):
        target[...] = lines[row : row + 1]
    expand_bias[...] = jnp.concatenate([early[6 + part : 7 + part] for part in range(parts)], axis=1)
    images = near_in.shape[0]
    for image in range(images):
        patch[y * images + image] = near_in[image] * inverse
        patch[(1 - y) * images + image] = far_in[image].astype(F32) * inverse


def emit(parts, place, done, near_in, far_in, sums, late):
    images, quarter, width = near_in.shape
    hidden = parts * width

    def out(*shape):
        return jax.ShapeDtypeStruct(shape, F32)

    small = out(1, 96)
    outs = [
        out(1, 1), small, small, out(96, 3 * width), small, small, out(96, width), small, small,
        small, out(96, hidden), out(1, hidden // 8), out(hidden // 8, width), small, out(96, width), small, small,
        out(2 * images, quarter, width),
    ]
    whole = pl.BlockSpec(memory_space=pltpu.VMEM)
    return pl.pallas_call(
        partial(emit_kernel, parts),
        in_specs=[pl.BlockSpec(memory_space=pltpu.SMEM)] + [whole] * 5,
        out_specs=[whole] * len(outs),
        out_shape=outs,
        compiler_params=params(60),
        cost_estimate=cost(1e6, 12e6),
        name="emit",
    )(place, done, near_in, far_in, sums, late)


def eight_places(
    patches,
    targets,
    mask_order,
    mask_count,
    attend_gain,
    attend_shift,
    joint_weight,
    query_bias,
    value_bias,
    output_weight,
    output_bias,
    feed_gain,
    feed_shift,
    expand_weight,
    expand_bias,
    reduce_weight,
    reduce_bias,
    pixel_weight,
    pixel_bias,
    mask_token,
):
    images, quarter, features = patches.shape
    near = images // 2
    place_y = own_bit("seq", 2)
    hidden = expand_bias.shape[0]
    parts = hidden // features

    def halves(values):
        return values.reshape((2, near) + values.shape[1:])

    lines = stack_lines(
        attend_gain,
        attend_shift,
        query_bias,
        value_bias,
        output_bias,
        feed_gain,
        feed_shift,
        reduce_bias,
        pixel_bias,
        mask_token,
        expand_bias,
    )
    orders = jnp.pad(mask_order[:, None, :], ((0, 0), (0, 7), (0, 256 - quarter)))
    reduce_parts = reduce_weight.reshape(8, parts, hidden // (8 * parts), features)
    place = jnp.stack([lax.axis_index("dp"), place_y]).astype(jnp.int32)
    embedded, input_one, joint, pairs, mixed, probs, mask, targets_here, weights = front(
        mask_count,
        halves(patches),
        halves(targets),
        halves(orders),
        lines,
        joint_weight,
        pixel_weight,
        expand_weight,
        output_weight,
    )
    lefts, rights, input_two, scaling_two, sums = middle(
        embedded, mixed, mask, targets_here, weights, reduce_parts, lines
    )
    done, patch_near, patch_far, sums, late = back(
        lefts,
        rights,
        weights,
        reduce_parts,
        joint_weight,
        input_two,
        scaling_two,
        input_one,
        joint,
        pairs,
        probs,
        lines,
        sums,
        embedded,
        mask,
    )
    outs = emit(parts, place, done, patch_near, patch_far, sums, late)
    flat = {0: (), 1: (-1,), 2: (-1,), 4: (-1,), 5: (-1,), 7: (-1,), 8: (-1,), 9: (-1,), 11: (-1,)}
    flat.update({13: (-1,), 15: (-1,), 16: (-1,)})
    return tuple(
        out.reshape(flat[index]) if index in flat else out for index, out in enumerate(outs)
    )


def on_device(*arguments):
    if lax.axis_size("dp") == 8 and lax.axis_size("seq") == 4:
        return eight_places(*arguments)
    return any_places(*arguments)


def solution(mesh):
    placed = (
        P("dp", "seq", None),
        P("dp", "seq", None),
        P("dp", "seq"),
        P("dp"),
        P(),
        P(),
        P(),
        P(),
        P(),
        P(),
        P(),
        P(),
        P(),
        P(),
        P(),
        P(),
        P(),
        P(),
        P(),
        P(),
    )
    return jax.shard_map(
        on_device,
        mesh=mesh,
        in_specs=placed,
        out_specs=(
            P(),
            P("dp"),
            P("dp"),
            P("dp", None),
            P("dp"),
            P("dp"),
            P("dp", None),
            P("dp"),
            P("dp"),
            P("dp"),
            P("dp", None),
            P("dp"),
            P("dp", None),
            P("dp"),
            P("dp", None),
            P("dp"),
            P("dp"),
            P("dp", "seq", None),
        ),
        check_vma=False,
    )
```

time: 1140 us -> 232 us (0.20); the launches traced: 1130 us -> 231 us
  waiting for transfers between devices: 589 us -> 0 us
  Pallas kernels: 0 us -> 227 us
  matrix products: 177 us -> 0 us
  local copies, waits for them, and re-layouts: 148 us -> 1.33 us
  other arithmetic: 91 us -> 1.86 us
  blocking collectives: 84.1 us -> 0 us
  starting transfers between devices: 20.4 us -> 0 us
  between operations: 18.5 us -> 0.71 us
    reduce_scatter x5 -> x0, waiting for transfers between devices: 413 us -> none  [the longest x1 164 us: on_device(): lax.psum_scatter(expand_weight_grad, 'dp', scatter_dimension=0, tiled=True)]
    pallas_call x0 -> x5, Pallas kernels: none -> 227 us  [the longest x1 145 us: back(): pl.pallas_call(partial(back_kernel, counts), grid=(FIRST_NORM + near,), i...]
    dot_general x57 -> x0, matrix products: 177 us -> none  [the longest x5 41.2 us: back_product(): jnp.einsum('rb,ab->ra', left, right, preferred_element_type=jnp.float32)]
    all_to_all x4 -> x0, waiting for transfers between devices: 176 us -> none  [the longest x1 75.9 us: on_device(): lax.all_to_all(grad_joint_heads.reshape(images, full_len, 3, 1, head_bloc...]
    reshape x10 -> x0, local copies, waits for them, and re-layouts: 71.1 us -> none  [the longest x2 16.5 us: on_device(): joint = joint.reshape(images, quarter, 3, seq_count, head_block)]
    convert_element_type x41 -> x0, other arithmetic: 53.5 us -> none  [the longest x2 6.15 us: on_device(): (normed_one * gain_one + attend_shift.astype(jnp.float32)).astype(jnp.bfl...]
    psum x2 -> x0, blocking collectives: 47.4 us -> none  [the longest x1 40.9 us: on_device(): lax.psum((channel_sums, jnp.sum(mask_float)), ('dp', 'seq'))]
    unnamed x1 -> x0, blocking collectives: 36.7 us -> none
  transfers between devices with their start and end apart: 10 -> 0, of which waited for: 7 -> 0; matrix products, arithmetic and copies ran while one was open for 21% -> 0% of each run, Pallas kernels for 0% -> 0%
where the time goes in v1:
time: 232 us; the launch traced here: 231 us
  Pallas kernels  227 us (98%)
    pallas_call x1, Pallas kernels, back(): pl.pallas_call(partial(back_kernel, counts), grid=(FIRST_NORM + near,), i...  145 us
    pallas_call x1, Pallas kernels, front(): pl.pallas_call(partial(front_kernel, parts), grid=(FRONT_ATTEND + near *...  47.4 us
    pallas_call x1, Pallas kernels, middle(): pl.pallas_call(middle_kernel, grid=(near,), in_specs=[block, block, colum...  27.7 us
    pallas_call x1, Pallas kernels, emit(): pl.pallas_call(partial(emit_kernel, parts), in_specs=[pl.BlockSpec(memory...  5.5 us

profile of v1, /device:TPU:0, one launch (start us, length us, event | category | flops | bytes accessed | tf_op | source)
XLA Modules:
  0.0 231.2 jit_solution(536313086965460748)
XLA Ops:
  0.7 1.5 stack_lines.1.lines
  2.2 0.7 copy.39
  2.9 0.6 pad.4.clone
  3.5 47.4 %front.1 = (bf16[3,288,768]{2,1,0:T(8,128)(2,1)}, bf16[3,288,768]{2,1,0:T(8,128)(2,1)}, bf16[3,6,3,288,128]{4,3,2,1,0:T(8,128)(2,1)}, bf16[3,6,2,288,128]{4,3,2,...) custom-call(s32[6]{0:T(128)} %counts.1, ...), custom_call_target="tpu_custom_call" | custom-call | flops 5000000000 | bytes 40000000 | tf_op jit(solution)/shard_map/front/pallas_call | solution.py:1224
  50.9 27.7 %middle.1 = (bf16[3,6,288,768]{3,2,1,0:T(8,128)(2,1)}, bf16[3,6,288,768]{3,2,1,0:T(8,128)(2,1)}, bf16[3,288,768]{2,1,0:T(8,128)(2,1)}, f32[3,288,1]{2,1,0:T(8,128)}, f32[16,768]{1,0:T(8,128)}) custom-call(bf16[3,288,768]{2,1,0:T(8,128)(2,1)} %get-tuple-element.55.embedded_in, bf16[3,288,768]{2,1,0:T(8,128)(2,1)} %get-tuple-element.56.mixed, ...), custom_call_target="tpu_custom_call" | custom-call | flops 10192158720 | bytes 40000000 | tf_op jit(solution)/shard_map/middle/pallas_call | solution.py:1338
  78.6 145.3 %back.1 = (bf16[13,2,2,48,384]{4,3,2,1,0:T(8,128)(2,1)}, f32[3,144,768]{2,1,0:T(8,128)}, bf16[3,144,768]{2,1,0:T(8,128)(2,1)}, f32[16,768]{1,0:T(8,128)}, f32[8,768]{1,0:T(8,128)}) custom-call(bf16[3,6,288,768]{3,2,1,0:T(8,128)(2,1)} %get-tuple-element.60.left, bf16[3,6,288,768]{3,2,1,0:T(8,128)(2,1)} %get-tuple-element.61.right, ...), custom_call_target="tpu_custom_call" | custom-call | flops 40000000000 | bytes 60000000 | tf_op jit(solution)/shard_map/back/pallas_call | solution.py:1707
  223.9 0.6 pad_add_fusion.place
  224.4 5.5 %emit.1 = (f32[1,1]{1,0:T(1,128)}, f32[1,96]{1,0:T(1,128)}, f32[1,96]{1,0:T(1,128)}, f32[96,2304]{1,0:T(8,128)}, f32[1,96]{1,0:T(1,128)}, /*index=5*/f32[1,96]{1...) custom-call(s32[2]{0:T(128)} %pad_add_fusion.place, ...), custom_call_target="tpu_custom_call" | custom-call | flops 1000000 | bytes 12000000 | tf_op jit(solution)/shard_map/emit/pallas_call | solution.py:1864
  229.9 1.3 reduce

commit v2 on v1

--- a/solution.py
+++ b/solution.py
@@ -804,6 +804,11 @@
 NAMES = ("high", "low", "x", "y")
 
 
+def names_of(order):
+    halved = [token for token in order if token in NAMES]
+    return tuple(halved + [name for name in NAMES if name not in halved])
+
+
 def stage_shapes(names, order, tail):
     names, shapes = list(names), []
     for token in order:
@@ -870,7 +875,7 @@
                 names.remove(token)
             self.names.append(names)
 
-    def copies(self, stage):
+    def copy(self, stage):
         token = self.order[stage]
         source, target = self.refs[stage], self.refs[stage + 1]
         if token[0] == "+":
@@ -882,23 +887,14 @@
             place, partner = self.where[token]
             dim = self.names[stage].index(token)
             source = source.at[(slice(None),) * dim + (1 - place,)]
-        base = 2 * (self.base + stage)
-        if len(source.shape) > 2:
-            pairs = [(source.at[half], target.at[half]) for half in range(2)]
-        else:
-            pairs = [(source, target)]
-        return [
-            remote(one, other, self.send.at[base + index], self.receive.at[base + index], partner)
-            for index, (one, other) in enumerate(pairs)
-        ]
+        spot = self.base + stage
+        return remote(source, target, self.send.at[spot], self.receive.at[spot], partner)
 
     def start(self, stage):
-        for copy in self.copies(stage):
-            copy.start()
+        self.copy(stage).start()
 
     def finish(self, stage):
-        for copy in self.copies(stage):
-            copy.wait()
+        self.copy(stage).wait()
         token = self.order[stage]
         source, target = self.refs[stage], self.refs[stage + 1]
         if token[0] == "G":
@@ -930,85 +926,84 @@
 MOST = 6
 TILE_ORDERS = (
     X_FIRST,
+    X_FIRST,
+    X_FIRST,
+    X_FIRST,
+    X_FIRST,
     Y_FIRST,
     Y_THEN_LOW,
-    Y_THEN_LOW,
     Y_FIRST,
+    X_FIRST,
     Y_FIRST,
     Y_FIRST,
     X_FIRST,
     X_FIRST,
-    Y_THEN_LOW,
-    Y_FIRST,
-    Y_FIRST,
-    X_FIRST,
 )
 TILE_SWAPS = (
     ("x", "low"),
+    ("x", "low"),
+    ("x", "low"),
+    ("x", "low"),
+    ("x", "low"),
     ("x", "y"),
     ("y", "low"),
-    ("y", "low"),
     ("x", "y"),
+    ("x", "low"),
     ("x", "y"),
     ("x", "y"),
     ("x", "low"),
     ("x", "low"),
-    ("y", "low"),
-    ("x", "y"),
-    ("x", "y"),
-    ("x", "low"),
 )
 TILES = len(TILE_ORDERS)
-TILE_STEPS = (0, 1, 2, 3, 4, 5, 6, 7, 8, 10, 18, 25, 31)
+TILE_STEPS = (0, 1, 2, 3, 4, 5, 6, 7, 8, 10, 15, 19, 22)
 TURNS = {
     2: ((0, 0),),
     3: ((1, 0),),
     4: ((0, 1), (2, 0),),
-    5: ((1, 1), (3, 0),),
+    5: ((3, 0), (1, 1),),
     6: ((0, 2), (4, 0),),
-    7: ((1, 2), (2, 1), (5, 0),),
-    8: ((0, 3), (3, 1), (6, 0),),
-    9: ((1, 3), (7, 0),),
-    10: ((0, 4), (1, 4), (2, 2), (4, 1), (8, 0),),
-    11: ((0, 5), (3, 2), (7, 1), (13, 0),),
-    12: ((9, 0), (1, 5), (2, 3), (5, 1), (13, 1), (6, 1),),
-    14: ((1, 6), (3, 3),),
-    15: ((2, 4), (4, 2),),
-    16: ((7, 2), (13, 2),),
-    17: ((3, 4),),
-    18: ((2, 5), (4, 3), (5, 2),),
-    19: ((2, 6), (3, 5), (7, 3), (13, 3), (6, 2), (8, 1), (9, 1),),
-    20: ((4, 4), (5, 3), (10, 0), (3, 6),),
-    21: ((7, 4), (13, 4),),
-    22: ((4, 5), (5, 4),),
-    23: ((7, 5), (6, 3),),
-    24: ((4, 6), (13, 5),),
-    25: ((5, 5), (8, 2), (9, 2), (10, 1),),
-    26: ((5, 6), (6, 4),),
-    27: ((9, 3), (11, 0), (6, 5), (8, 3), (10, 2),),
-    28: ((9, 4),),
-    29: ((6, 6),),
-    30: ((10, 3),),
-    31: ((9, 5), (8, 4),),
-    32: ((9, 6), (8, 5), (10, 4), (11, 1),),
-    33: ((12, 0), (10, 5),),
+    7: ((5, 0),),
+    8: ((1, 2), (6, 0), (0, 3), (2, 1),),
+    9: ((7, 0),),
+    10: ((0, 4), (1, 3), (3, 1), (8, 0),),
+    11: ((0, 5), (5, 1), (13, 0), (4, 1),),
+    12: ((1, 4), (2, 2), (13, 1), (9, 0),),
+    13: ((1, 5),),
+    14: ((3, 2), (13, 2), (6, 1), (7, 1),),
+    15: ((2, 3), (4, 2), (5, 2),),
+    16: ((13, 3),),
+    17: ((2, 4), (3, 3), (7, 2), (8, 1), (10, 0), (9, 1), (4, 3),),
+    18: ((2, 5), (13, 4), (5, 3), (6, 2),),
+    19: ((3, 4), (7, 3), (8, 2),),
+    20: ((3, 5), (4, 4), (9, 2), (6, 3),),
+    21: ((4, 5), (13, 5), (5, 4), (10, 1), (11, 0),),
+    22: ((7, 4), (9, 3),),
+    23: ((5, 5), (7, 5), (6, 4), (8, 3), (10, 2),),
+    24: ((9, 4), (11, 1), (12, 0), (5, 6), (7, 6),),
+    25: ((6, 5), (10, 3),),
 }
 LAST_TURNS = (
     (14, 0),
+    (11, 2),
+    (9, 5),
+    (6, 6),
+    (8, 4),
+    (14, 1),
+    (9, 6),
+    (8, 5),
+    (10, 4),
+    (14, 2),
+    (11, 3),
+    (12, 1),
+    (14, 3),
+    (10, 5),
+    (12, 2),
     (10, 6),
-    (14, 1),
-    (11, 2),
-    (12, 1),
-    (11, 3),
-    (14, 2),
-    (12, 2),
-    (14, 3),
+    (14, 4),
     (11, 4),
-    (14, 4),
+    (14, 5),
+    (11, 5),
     (12, 3),
-    (11, 5),
-    (14, 5),
-    (11, 6),
     (12, 4),
     (12, 5),
 )
@@ -1035,6 +1030,7 @@
 FRONT_OWN = 6
 FRONT_FAR = 9
 FRONT_ATTEND = 12
+FRONT_PAIRS = 2
 
 
 def lines_kernel(*refs):
@@ -1175,25 +1171,31 @@
         joint_out[0] = joint[image]
         masks_out[0] = masks[image]
 
-    @pl.when(step >= FRONT_ATTEND)
-    def _():
-        place = step - FRONT_ATTEND
-        image, pair = lax.div(place, heads), lax.rem(place, heads)
-
-        @pl.when(pair == 0)
-        def _():
-            pair_copy(image).wait()
-
+    def attend(image, pair, index):
         queries = side_by_side(joint[image, pair, 0] * jnp.asarray(HEAD_DIM**-0.5, BF16))
         keys_in = jnp.concatenate([joint[image, pair, 1], pairs[image, pair, 0]], axis=0)
         values_in = jnp.concatenate([joint[image, pair, 2], pairs[image, pair, 1]], axis=0)
-        pairs_out[0, 0] = pairs[image, pair]
+        pairs_out[0, index] = pairs[image, pair]
         scores = dot_nt(keys_in, queries)
         exponent = jnp.exp(scores - jnp.max(scores, axis=0, keepdims=True))
         total = jnp.sum(exponent, axis=0, keepdims=True)
         probs = (exponent * (1.0 / total)).astype(BF16)
-        probs_out[0, 0] = probs
-        mixed_out[0] = merge_turned(dot_tn(values_in, probs)).astype(BF16)
+        probs_out[0, index] = probs
+        mixed = merge_turned(dot_tn(values_in, probs)).astype(BF16)
+        mixed_out[0, :, index * PAIR : (index + 1) * PAIR] = mixed
+
+    @pl.when(step >= FRONT_ATTEND)
+    def _():
+        place = step - FRONT_ATTEND
+        turns = heads // FRONT_PAIRS
+        image, turn = lax.div(place, turns), lax.rem(place, turns)
+
+        @pl.when(turn == 0)
+        def _():
+            pair_copy(image).wait()
+
+        for index in range(FRONT_PAIRS):
+            attend(image, turn * FRONT_PAIRS + index, index)
 
     @pl.when(step == pl.num_programs(0) - 1)
     def _():
@@ -1216,14 +1218,16 @@
     def image(step):
         return jnp.clip(step - FRONT_FAR, 0, near - 1)
 
+    turns = heads // FRONT_PAIRS
+
     def spot(step):
         place = jnp.maximum(step - FRONT_ATTEND, 0)
-        return lax.div(place, heads), lax.rem(place, heads)
+        return lax.div(place, turns), lax.rem(place, turns)
 
     block = pl.BlockSpec((1, rows, width), lambda s: (image(s), 0, 0))
     return pl.pallas_call(
         partial(front_kernel, parts),
-        grid=(FRONT_ATTEND + near * heads,),
+        grid=(FRONT_ATTEND + near * turns,),
         in_specs=[
             pl.BlockSpec(memory_space=pltpu.SMEM),
             pl.BlockSpec(memory_space=pl.ANY),
@@ -1236,9 +1240,9 @@
             block,
             block,
             pl.BlockSpec((1, heads, 3, rows, PAIR), lambda s: (image(s), 0, 0, 0, 0)),
-            pl.BlockSpec((1, 1, 2, rows, PAIR), lambda s: spot(s) + (0, 0, 0)),
-            pl.BlockSpec((1, rows, PAIR), lambda s: (spot(s)[0], 0, spot(s)[1])),
-            pl.BlockSpec((1, 1, 2 * rows, 2 * rows), lambda s: spot(s) + (0, 0)),
+            pl.BlockSpec((1, FRONT_PAIRS, 2, rows, PAIR), lambda s: spot(s) + (0, 0, 0)),
+            pl.BlockSpec((1, rows, FRONT_PAIRS * PAIR), lambda s: (spot(s)[0], 0, spot(s)[1])),
+            pl.BlockSpec((1, FRONT_PAIRS, 2 * rows, 2 * rows), lambda s: spot(s) + (0, 0)),
             pl.BlockSpec((1, rows, 1), lambda s: (image(s), 0, 0)),
             pl.BlockSpec(memory_space=pl.ANY),
             pl.BlockSpec((1, width, width), lambda s: (jnp.minimum(s, parts + 1), 0, 0)),
@@ -1369,7 +1373,7 @@
 HIGH_ROWS = 4 * 96
 
 
-def spread_half(result, target, high, start, swapped):
+def spread_half(result, target, high, start, names, swapped):
     for low in range(2):
         for x in range(2):
             for y in range(2):
@@ -1379,15 +1383,15 @@
                 if swapped is not None:
                     first, second = swapped
                     spot[first], spot[second] = spot[second], spot[first]
-                target[tuple(spot[name] for name in NAMES)] = piece.astype(BF16)
+                target[tuple(spot[name] for name in names)] = piece.astype(BF16)
 
 
 HALF = 48
 SLOTS = 4
 KEPT = 10
 FIRST_ATTEND = 11
-GROUP_STEPS = (18, 25, 31)
-FIRST_NORM = 32
+GROUP_STEPS = (15, 19, 22)
+FIRST_NORM = 23
 
 
 def back_kernel(
@@ -1400,6 +1404,8 @@
         far_out,
         sums_out,
         late_out,
+        done,
+        done_sent,
         branch,
         wide,
         grad_in,
@@ -1421,8 +1427,8 @@
         pair_receive,
         far_send,
         far_receive,
-    ) = rest[:26]
-    buffers = split_list(rest[26:], counts)
+    ) = rest[:28]
+    buffers = split_list(rest[28:], counts)
     where = places()
     core, sibling = where["core"]
     step = pl.program_id(0)
@@ -1432,7 +1438,7 @@
     heads = width // PAIR
     first_gain, second_gain = lines[GAIN_ONE : GAIN_ONE + 1], lines[GAIN_TWO : GAIN_TWO + 1]
     chains = [
-        Chain(where, keep.at[unit % KEPT], NAMES, order, buffers[unit], send, receive, MOST * unit, TILE_SWAPS[unit])
+        Chain(where, keep.at[unit % KEPT], names_of(order), order, list(buffers[unit]) + [done.at[unit]], send, receive, MOST * unit, TILE_SWAPS[unit])
         for unit, order in enumerate(TILE_ORDERS)
     ]
     chains.append(Chain(where, sums, (), SUMS_ORDER, buffers[TILES], send, receive, MOST * TILES))
@@ -1442,8 +1448,9 @@
         slot = lax.rem(unit, SLOTS)
         return remote(give.at[slot], got.at[slot], core_send.at[unit], core_receive.at[unit], sibling)
 
-    def pair_copy(place):
-        slot = lax.rem(place, SLOTS)
+    def pair_copy(place, second):
+        image = lax.rem(place, 3)
+        slot = lax.rem((lax.div(place, 6) * 3 + image) * 2 + second, SLOTS)
         return remote(
             give_pairs.at[slot], got_pairs.at[place], pair_send.at[place], pair_receive.at[place], sibling
         )
@@ -1456,48 +1463,45 @@
     def core_sum(unit):
         core_copy(unit).wait()
         for_each(4, lambda spot: add_up(keep.at[unit % KEPT], spot, got[(unit % SLOTS,) + spot]))
+
+    def done_copy(unit):
+        return pltpu.make_async_copy(done.at[unit], done_out.at[unit], done_sent.at[unit])
 
     def turn(unit, stage):
         if unit < TILES and stage == 0:
             core_sum(unit)
         chains[unit].turn(stage)
         if stage == len(chains[unit].order) and unit < TILES:
-            done_out[unit] = chains[unit].refs[-1][...]
-
-    def tile(unit, lines_of, value, swaps):
-        def one(high, carry):
-            columns = pl.ds(pl.multiple_of(high * HIGH_ROWS, HIGH_ROWS), HIGH_ROWS)
+            done_copy(unit).start()
+
+    def tile(unit, lines_of, value, forms):
+        def one(high):
+            columns = slice(high * HIGH_ROWS, (high + 1) * HIGH_ROWS)
             result = dot_tn(lines_of(columns).reshape(every, HIGH_ROWS), value)
             for half in range(2):
-                for swapped, chosen in [(None, True)] if half == 0 else swaps:
+                for names, swapped, chosen in forms:
+                    swapped = swapped if half == 1 else None
 
                     @pl.when(jnp.logical_and(core == half, chosen))
-                    def _(half=half, swapped=swapped):
-                        spread_half(result, keep.at[lax.rem(unit, KEPT)], high, half * HALF, swapped)
+                    def _(half=half, names=names, swapped=swapped):
+                        spread_half(result, keep.at[lax.rem(unit, KEPT)], high, half * HALF, names, swapped)
 
                     @pl.when(jnp.logical_and(core != half, chosen))
-                    def _(half=half, swapped=swapped):
-                        spread_half(result, give.at[lax.rem(unit, SLOTS)], high, half * HALF, swapped)
-
-            return carry
-
-        lax.fori_loop(0, 2, one, 0)
+                    def _(half=half, names=names, swapped=swapped):
+                        spread_half(result, give.at[lax.rem(unit, SLOTS)], high, half * HALF, names, swapped)
+
+        for high in range(2):
+            one(high)
         core_copy(unit).start()
 
-    def swaps_of(units, unit):
-        kinds = []
+    def forms_of(units, unit):
+        forms = {}
         for other in units:
-            if TILE_SWAPS[other] not in kinds:
-                kinds.append(TILE_SWAPS[other])
-        if len(kinds) == 1:
-            return [(kinds[0], True)]
-        found = []
-        for kind in kinds:
-            chosen = functools.reduce(
-                jnp.logical_or, [unit == other for other in units if TILE_SWAPS[other] == kind]
-            )
-            found.append((kind, chosen))
-        return found
+            form = (names_of(TILE_ORDERS[other]), TILE_SWAPS[other])
+            forms.setdefault(form, []).append(unit == other)
+        if len(forms) == 1:
+            return [form + (True,) for form in forms]
+        return [form + (functools.reduce(jnp.logical_or, asked),) for form, asked in forms.items()]
 
     def flat(ref):
         return ref[...].reshape(every, ref.shape[-1])
@@ -1521,44 +1525,41 @@
 
     @pl.when(step == 0)
     def _():
-        tile(0, left_lines, right[:, 0].reshape(every, width), swaps_of((0,), 0))
-
-        def one(image, carry):
+        tile(0, left_lines, right[:, 0].reshape(every, width), forms_of((0,), 0))
+
+        def one(image):
             low = dot_nt(right[image, 0], weights[0]).astype(BF16)
             branch[image] = low
             sums[1:2] += column_sums(low)
-            return carry
-
-        lax.fori_loop(0, images, one, 0)
+        for image in range(images):
+            one(image)
 
     @pl.when((step > 0) & (step < 9) & (lax.rem(step, 2) == 1))
     def _():
-        tile(step, left_lines, flat(branch), swaps_of((1, 3, 5, 7), step))
+        tile(step, left_lines, flat(branch), forms_of((1, 3, 5, 7), step))
         row = pl.ds(6 + lax.div(step, 2), 1)
 
-        def one(image, carry):
+        def one(image):
             low = dot_nt(branch[image], reduce[:, 0].reshape(width, width)) * right[image, 0].astype(F32)
             low = low.astype(BF16)
             wide[image] = low
             sums[row] += column_sums(low)
-            return carry
-
-        lax.fori_loop(0, images, one, 0)
+        for image in range(images):
+            one(image)
 
     @pl.when((step > 0) & (step < 9) & (lax.rem(step, 2) == 0))
     def _():
-        tile(step, lambda columns: input_two[:, :, columns], flat(wide), swaps_of((2, 4, 6, 8), step))
+        tile(step, lambda columns: input_two[:, :, columns], flat(wide), forms_of((2, 4, 6, 8), step))
         fresh = jnp.where(step == 2, 0.0, 1.0)
 
-        def one(image, carry):
+        def one(image):
             grad_in[image] = grad_in[image] * fresh + dot_nt(wide[image], weights[0])
-            return carry
-
-        lax.fori_loop(0, images, one, 0)
+        for image in range(images):
+            one(image)
 
     @pl.when(step == 9)
     def _():
-        def one(image, carry):
+        def one(image):
             normed = right[image, 0].astype(F32)
             grad = grad_in[image]
             low = branch[image].astype(F32) + normalize_back(grad, normed, scaling_two[image], second_gain)
@@ -1570,34 +1571,29 @@
             mixed = dot_nt(low, weights[0]).astype(BF16)
             for pair in range(heads):
                 upstream[image, pair] = mixed[:, pair * PAIR : (pair + 1) * PAIR]
-            return carry
-
-        lax.fori_loop(0, images, one, 0)
+        for image in range(images):
+            one(image)
 
     @pl.when(step == 10)
     def _():
-        tile(9, left_lines, flat(branch), swaps_of((9,), 9))
-
-    attends = (step >= FIRST_ATTEND) & (step < GROUP_STEPS[2]) & (step != GROUP_STEPS[0]) & (step != GROUP_STEPS[1])
-
-    @pl.when(attends)
-    def _():
-        place = attend_place(step)
-        group, inside = lax.div(place, 6), lax.rem(place, 6)
-        image, pair = lax.rem(inside, 3), group * 2 + lax.div(inside, 3)
-
-        @pl.when(place >= SLOTS)
+        tile(9, left_lines, flat(branch), forms_of((9,), 9))
+
+    def attend_back(group, image, second, inside, order):
+        place = group * 6 + inside
+
+        @pl.when(order >= SLOTS)
         def _():
-            pair_copy(place - SLOTS).wait_send()
+            before = order - SLOTS
+            pair_copy(lax.div(before, 6) * 6 + second * 3 + lax.rem(lax.div(before, 2), 3), second).wait_send()
 
         scale = HEAD_DIM**-0.5
         target = own_pairs.at[lax.rem(group, 2), inside]
-        away = give_pairs.at[lax.rem(place, SLOTS)]
-        queries = side_by_side(joint[0, 0, 0])
-        keys_in = jnp.concatenate([joint[0, 0, 1], pairs[0, 0, 0]], axis=0)
-        values_in = jnp.concatenate([joint[0, 0, 2], pairs[0, 0, 1]], axis=0)
-        grad_mixed = side_by_side(upstream[image, pair])
-        probs = probs_in[0, 0]
+        away = give_pairs.at[lax.rem(order, SLOTS)]
+        queries = side_by_side(joint[0, second, 0])
+        keys_in = jnp.concatenate([joint[0, second, 1], pairs[0, second, 0]], axis=0)
+        values_in = jnp.concatenate([joint[0, second, 2], pairs[0, second, 1]], axis=0)
+        grad_mixed = side_by_side(upstream[image, group * 2 + second])
+        probs = probs_in[0, second]
         grad_probs = dot_nt(values_in, grad_mixed)
         broad = probs.astype(F32)
         weighted = broad * grad_probs
@@ -1610,14 +1606,23 @@
         target[2] = grad_values[:rows]
         away[0] = grad_keys[rows:]
         away[1] = grad_values[rows:]
-        pair_copy(place).start()
+        pair_copy(place, second).start()
+
+    attends = (step >= FIRST_ATTEND) & (step < GROUP_STEPS[2]) & (step != GROUP_STEPS[0]) & (step != GROUP_STEPS[1])
+
+    @pl.when(attends)
+    def _():
+        group, image = attend_place(step)
+        for second in range(2):
+            inside = second * 3 + image
+            attend_back(group, image, second, inside, (group * 3 + image) * 2 + second)
 
     @pl.when((step == GROUP_STEPS[0]) | (step == GROUP_STEPS[1]) | (step == GROUP_STEPS[2]))
     def _():
         group = jnp.where(step == GROUP_STEPS[0], 0, jnp.where(step == GROUP_STEPS[1], 1, 2))
         slot = lax.rem(group, 2)
         for inside in range(6):
-            pair_copy(group * 6 + inside).wait_recv()
+            pair_copy(group * 6 + inside, inside // 3).wait_recv()
             image, second = inside % 3, inside // 3
             for part in range(3):
                 piece = own_pairs[slot, inside, part]
@@ -1625,17 +1630,16 @@
                     piece = piece.astype(F32) + got_pairs[group * 6 + inside, part - 1].astype(F32)
                 start = part * 2 * PAIR + second * PAIR
                 wide[image, :, start : start + PAIR] = piece.astype(BF16)
-        tile(10 + group, lambda columns: input_one[:, :, columns], flat(wide), swaps_of((10, 11, 12), 10 + group))
+        tile(10 + group, lambda columns: input_one[:, :, columns], flat(wide), forms_of((10, 11, 12), 10 + group))
         columns = jnp.concatenate([query[...], key[...], value[...]], axis=1)
         fresh = jnp.where(group == 0, 0.0, 1.0)
         row = pl.ds(5 + group, 1)
 
-        def one(image, carry):
+        def one(image):
             late[row] += column_sums(wide[image])
             grad_in[image] = grad_in[image] * fresh + dot_nt(wide[image], columns)
-            return carry
-
-        lax.fori_loop(0, images, one, 0)
+        for image in range(images):
+            one(image)
 
     @pl.when(step >= FIRST_NORM)
     def _():
@@ -1658,8 +1662,11 @@
             turn(unit, stage)
         for image in range(images):
             far_copy(image).wait()
-        for place in range(3 * heads - SLOTS, 3 * heads):
-            pair_copy(place).wait_send()
+        for unit in range(TILES):
+            done_copy(unit).wait()
+        for image in range(1, 3):
+            for second in range(2):
+                pair_copy(12 + second * 3 + image, second).wait_send()
         sums_out[...] = chains[TILES].refs[-1][...]
         late_out[...] = chains[TILES + 1].refs[-1][...]
 
@@ -1668,7 +1675,8 @@
     place = step - FIRST_ATTEND
     for at in GROUP_STEPS[:2]:
         place = place - jnp.where(step > at, 1, 0)
-    return jnp.clip(place, 0, 17)
+    place = jnp.clip(place, 0, 8)
+    return lax.div(place, 3), lax.rem(place, 3)
 
 
 def back(
@@ -1691,17 +1699,21 @@
         return pl.BlockSpec((width, 2 * PAIR), lambda s: (0, which * 3 + group(s)))
 
     def spot(step):
-        place = attend_place(step)
-        group, inside = lax.div(place, 6), lax.rem(place, 6)
-        return lax.rem(inside, 3), group * 2 + lax.div(inside, 3)
+        group, image = attend_place(step)
+        return image, group
 
     def image(step):
         return jnp.maximum(step - FIRST_NORM, 0)
 
-    cases = [(NAMES, order, (HALF, 384), BF16) for order in TILE_ORDERS]
+    cases = [(names_of(order), order, (HALF, 384), BF16) for order in TILE_ORDERS]
     cases.append(((), SUMS_ORDER, sums.shape, F32))
     cases.append(((), SUMS_ORDER, (8, width), F32))
     buffers, counts = chain_scratch(cases)
+    kept, start = [], 0
+    for index, count in enumerate(counts):
+        kept += buffers[start : start + count - (index < TILES)]
+        start += count
+    buffers, counts = kept, [count - (index < TILES) for index, count in enumerate(counts)]
     whole = (2, 2, 2, 2, HALF, 384)
     stack = pl.BlockSpec((near, 1, rows, width), lambda s: (0, slot(s), 0, 0))
     return pl.pallas_call(
@@ -1718,16 +1730,16 @@
             fixed((near, rows, width)),
             fixed((near, rows, 1)),
             fixed((near, rows, width)),
-            pl.BlockSpec((1, 1, 3, rows, PAIR), lambda s: spot(s) + (0, 0, 0)),
-            pl.BlockSpec((1, 1, 2, rows, PAIR), lambda s: spot(s) + (0, 0, 0)),
-            pl.BlockSpec((1, 1, 2 * rows, 2 * rows), lambda s: spot(s) + (0, 0)),
+            pl.BlockSpec((1, 2, 3, rows, PAIR), lambda s: spot(s) + (0, 0, 0)),
+            pl.BlockSpec((1, 2, 2, rows, PAIR), lambda s: spot(s) + (0, 0, 0)),
+            pl.BlockSpec((1, 2, 2 * rows, 2 * rows), lambda s: spot(s) + (0, 0)),
             fixed(lines.shape),
             fixed(sums.shape),
             pl.BlockSpec((1, rows, width), lambda s: (image(s), 0, 0)),
             pl.BlockSpec((1, rows, 1), lambda s: (image(s), 0, 0)),
         ],
         out_specs=[
-            fixed((TILES, 2, 2, HALF, 384)),
+            pl.BlockSpec(memory_space=pl.ANY),
             pl.BlockSpec((1, quarter, width), lambda s: (image(s), 0, 0)),
             pl.BlockSpec(memory_space=pl.ANY),
             fixed_out(sums.shape),
@@ -1741,6 +1753,8 @@
             jax.ShapeDtypeStruct((8, width), F32),
         ],
         scratch_shapes=[
+            pltpu.VMEM((TILES, 2, 2, HALF, 384), BF16),
+            pltpu.SemaphoreType.DMA((TILES,)),
             pltpu.VMEM((near, rows, width), BF16),
             pltpu.VMEM((near, rows, width), BF16),
             pltpu.VMEM((near, rows, width), F32),
@@ -1754,8 +1768,8 @@
             pltpu.VMEM((KEPT,) + whole, BF16),
             pltpu.VMEM((SLOTS,) + whole, BF16),
             pltpu.VMEM((SLOTS,) + whole, BF16),
-            pltpu.SemaphoreType.DMA((2 * MOST * (TILES + 2),)),
-            pltpu.SemaphoreType.DMA((2 * MOST * (TILES + 2),)),
+            pltpu.SemaphoreType.DMA((MOST * (TILES + 2),)),
+            pltpu.SemaphoreType.DMA((MOST * (TILES + 2),)),
             pltpu.SemaphoreType.DMA((TILES,)),
             pltpu.SemaphoreType.DMA((TILES,)),
             pltpu.SemaphoreType.DMA((near * heads,)),

time: 232 us -> 215 us (0.927)
  Pallas kernels: 227 us -> 211 us
    pallas_call x1, Pallas kernels: 145 us -> 133 us  [back(): pl.pallas_call(partial(back_kernel, counts), grid=(FIRST_NORM + near,), i...]
    pallas_call x1, Pallas kernels: 47.4 us -> 42.8 us  [front(): pl.pallas_call(partial(front_kernel, parts), grid=(FRONT_ATTEND + near *...]
where the time goes in v2:
time: 215 us
  Pallas kernels  211 us (98%)
    pallas_call x1, Pallas kernels, back(): pl.pallas_call(partial(back_kernel, counts), grid=(FIRST_NORM + near,), i...  133 us
    pallas_call x1, Pallas kernels, front(): pl.pallas_call(partial(front_kernel, parts), grid=(FRONT_ATTEND + near *...  42.8 us
    pallas_call x1, Pallas kernels, middle(): pl.pallas_call(middle_kernel, grid=(near,), in_specs=[block, block, colum...  27.8 us
    pallas_call x1, Pallas kernels, emit(): pl.pallas_call(partial(emit_kernel, parts), in_specs=[pl.BlockSpec(memory...  5.5 us

profile of v2, /device:TPU:0, one launch (start us, length us, event | category | flops | bytes accessed | tf_op | source)
XLA Modules:
  0.0 214.9 jit_solution(14535770681093010180)
XLA Ops:
  0.7 1.5 stack_lines.1.lines
  2.2 0.7 copy.39
  2.9 0.6 pad.4.clone
  3.5 42.8 %front.1 = (bf16[3,288,768]{2,1,0:T(8,128)(2,1)}, bf16[3,288,768]{2,1,0:T(8,128)(2,1)}, bf16[3,6,3,288,128]{4,3,2,1,0:T(8,128)(2,1)}, bf16[3,6,2,288,128]{4,3,2,...) custom-call(s32[6]{0:T(128)} %counts.1, ...), custom_call_target="tpu_custom_call" | custom-call | flops 5000000000 | bytes 40000000 | tf_op jit(solution)/shard_map/front/pallas_call | solution.py:1228
  46.3 27.8 %middle.1 = (bf16[3,6,288,768]{3,2,1,0:T(8,128)(2,1)}, bf16[3,6,288,768]{3,2,1,0:T(8,128)(2,1)}, bf16[3,288,768]{2,1,0:T(8,128)(2,1)}, f32[3,288,1]{2,1,0:T(8,128)}, f32[16,768]{1,0:T(8,128)}) custom-call(bf16[3,288,768]{2,1,0:T(8,128)(2,1)} %get-tuple-element.55.embedded_in, bf16[3,288,768]{2,1,0:T(8,128)(2,1)} %get-tuple-element.56.mixed, ...), custom_call_target="tpu_custom_call" | custom-call | flops 10192158720 | bytes 40000000 | tf_op jit(solution)/shard_map/middle/pallas_call | solution.py:1342
  74.1 133.4 %back.1 = (bf16[13,2,2,48,384]{4,3,2,1,0:T(8,128)(2,1)}, f32[3,144,768]{2,1,0:T(8,128)}, bf16[3,144,768]{2,1,0:T(8,128)(2,1)}, f32[16,768]{1,0:T(8,128)}, f32[8,768]{1,0:T(8,128)}) custom-call(bf16[3,6,288,768]{3,2,1,0:T(8,128)(2,1)} %get-tuple-element.60.left, bf16[3,6,288,768]{3,2,1,0:T(8,128)(2,1)} %get-tuple-element.61.right, ...), custom_call_target="tpu_custom_call" | custom-call | flops 40000000000 | bytes 60000000 | tf_op jit(solution)/shard_map/back/pallas_call | solution.py:1719
  207.6 0.6 pad_add_fusion.place
  208.2 5.5 %emit.1 = (f32[1,1]{1,0:T(1,128)}, f32[1,96]{1,0:T(1,128)}, f32[1,96]{1,0:T(1,128)}, f32[96,2304]{1,0:T(8,128)}, f32[1,96]{1,0:T(1,128)}, /*index=5*/f32[1,96]{1...) custom-call(s32[2]{0:T(128)} %pad_add_fusion.place, ...), custom_call_target="tpu_custom_call" | custom-call | flops 1000000 | bytes 12000000 | tf_op jit(solution)/shard_map/emit/pallas_call | solution.py:1878
  213.7 1.3 reduce

commit v3 on v2

--- a/solution.py
+++ b/solution.py
@@ -840,7 +840,7 @@
 
 
 def add_up(target, place, other):
-    target[place] = (target[place].astype(F32) + other.astype(F32)).astype(target.dtype)
+    target[place] = target[place] + other
 
 
 class Chain:
@@ -925,31 +925,31 @@
 SUMS_ORDER = ("+core", "+y", "+x", "+low", "+high")
 MOST = 6
 TILE_ORDERS = (
-    X_FIRST,
-    X_FIRST,
-    X_FIRST,
-    X_FIRST,
+    Y_FIRST,
+    Y_FIRST,
+    Y_THEN_LOW,
     X_FIRST,
     Y_FIRST,
+    Y_FIRST,
+    X_FIRST,
     Y_THEN_LOW,
     Y_FIRST,
-    X_FIRST,
-    Y_FIRST,
+    Y_THEN_LOW,
     Y_FIRST,
     X_FIRST,
     X_FIRST,
 )
 TILE_SWAPS = (
-    ("x", "low"),
-    ("x", "low"),
-    ("x", "low"),
-    ("x", "low"),
+    ("x", "y"),
+    ("x", "y"),
+    ("y", "low"),
     ("x", "low"),
     ("x", "y"),
+    ("x", "y"),
+    ("x", "low"),
     ("y", "low"),
     ("x", "y"),
-    ("x", "low"),
-    ("x", "y"),
+    ("y", "low"),
     ("x", "y"),
     ("x", "low"),
     ("x", "low"),
@@ -959,51 +959,52 @@
 TURNS = {
     2: ((0, 0),),
     3: ((1, 0),),
-    4: ((0, 1), (2, 0),),
-    5: ((3, 0), (1, 1),),
-    6: ((0, 2), (4, 0),),
-    7: ((5, 0),),
-    8: ((1, 2), (6, 0), (0, 3), (2, 1),),
-    9: ((7, 0),),
-    10: ((0, 4), (1, 3), (3, 1), (8, 0),),
-    11: ((0, 5), (5, 1), (13, 0), (4, 1),),
-    12: ((1, 4), (2, 2), (13, 1), (9, 0),),
-    13: ((1, 5),),
-    14: ((3, 2), (13, 2), (6, 1), (7, 1),),
-    15: ((2, 3), (4, 2), (5, 2),),
-    16: ((13, 3),),
-    17: ((2, 4), (3, 3), (7, 2), (8, 1), (10, 0), (9, 1), (4, 3),),
-    18: ((2, 5), (13, 4), (5, 3), (6, 2),),
-    19: ((3, 4), (7, 3), (8, 2),),
-    20: ((3, 5), (4, 4), (9, 2), (6, 3),),
-    21: ((4, 5), (13, 5), (5, 4), (10, 1), (11, 0),),
-    22: ((7, 4), (9, 3),),
-    23: ((5, 5), (7, 5), (6, 4), (8, 3), (10, 2),),
-    24: ((9, 4), (11, 1), (12, 0), (5, 6), (7, 6),),
-    25: ((6, 5), (10, 3),),
+    4: ((2, 0), (0, 1),),
+    5: ((3, 0),),
+    6: ((1, 1), (4, 0),),
+    7: ((0, 2), (2, 1), (5, 0),),
+    8: ((1, 2), (3, 1), (6, 0),),
+    9: ((0, 3), (7, 0),),
+    10: ((1, 3), (2, 2), (4, 1), (8, 0),),
+    11: ((0, 4), (5, 1), (13, 0),),
+    12: ((1, 4), (3, 2), (13, 1), (9, 0),),
+    13: ((0, 5), (2, 3),),
+    14: ((0, 6), (6, 1), (7, 1), (1, 5), (4, 2),),
+    15: ((1, 6), (2, 4), (3, 3), (13, 2),),
+    16: ((5, 2),),
+    17: ((2, 5), (4, 3), (13, 3), (8, 1), (10, 0),),
+    18: ((2, 6), (3, 4), (6, 2), (7, 2), (9, 1), (5, 3),),
+    19: ((3, 5), (4, 4), (13, 4),),
+    20: ((7, 3), (8, 2),),
+    21: ((4, 5), (5, 4), (9, 2), (10, 1), (11, 0),),
+    22: ((4, 6), (13, 5), (6, 3), (8, 3),),
+    23: ((5, 5), (7, 4), (9, 3),),
+    24: ((6, 4), (8, 4), (10, 2), (12, 0), (5, 6), (6, 5), (7, 5), (11, 1),),
+    25: ((9, 4),),
 }
 LAST_TURNS = (
     (14, 0),
+    (8, 5),
+    (10, 3),
+    (7, 6),
+    (14, 1),
+    (8, 6),
+    (10, 4),
+    (9, 5),
     (11, 2),
-    (9, 5),
-    (6, 6),
-    (8, 4),
-    (14, 1),
+    (14, 2),
     (9, 6),
-    (8, 5),
-    (10, 4),
-    (14, 2),
-    (11, 3),
     (12, 1),
     (14, 3),
     (10, 5),
+    (11, 3),
     (12, 2),
+    (14, 4),
     (10, 6),
-    (14, 4),
+    (14, 5),
+    (12, 3),
     (11, 4),
-    (14, 5),
     (11, 5),
-    (12, 3),
     (12, 4),
     (12, 5),
 )
@@ -1789,14 +1790,14 @@
     )
 
 
-def emit_kernel(parts, place, done, near_in, far_in, sums, late, *outs):
+def emit_kernel(parts, done, near_in, far_in, sums, late, *outs):
     (
         loss, attend_gain, attend_shift, joint, query_bias, value_bias, output, output_bias, feed_gain,
         feed_shift, expand, expand_bias, reduce, reduce_bias, pixel, pixel_bias, token, patch,
     ) = outs
-    data, y = place[0], place[1]
+    data, y = lax.axis_index("dp"), lax.div(lax.axis_index("seq"), 2)
     inverse = 1.0 / (sums[10:11] * PIXELS)
-    loss[...] = jnp.sum(sums[5:6] * inverse, axis=1, keepdims=True)
+    loss[0] = jnp.sum(sums[5:6] * inverse)
     wide_inverse = inverse[:, :384]
 
     def piece(unit, core, half):
@@ -1861,7 +1862,7 @@
         patch[(1 - y) * images + image] = far_in[image].astype(F32) * inverse
 
 
-def emit(parts, place, done, near_in, far_in, sums, late):
+def emit(parts, done, near_in, far_in, sums, late):
     images, quarter, width = near_in.shape
     hidden = parts * width
 
@@ -1870,20 +1871,20 @@
 
     small = out(1, 96)
     outs = [
-        out(1, 1), small, small, out(96, 3 * width), small, small, out(96, width), small, small,
+        out(1), small, small, out(96, 3 * width), small, small, out(96, width), small, small,
         small, out(96, hidden), out(1, hidden // 8), out(hidden // 8, width), small, out(96, width), small, small,
         out(2 * images, quarter, width),
     ]
     whole = pl.BlockSpec(memory_space=pltpu.VMEM)
     return pl.pallas_call(
         partial(emit_kernel, parts),
-        in_specs=[pl.BlockSpec(memory_space=pltpu.SMEM)] + [whole] * 5,
-        out_specs=[whole] * len(outs),
+        in_specs=[whole] * 5,
+        out_specs=[pl.BlockSpec(memory_space=pltpu.SMEM)] + [whole] * (len(outs) - 1),
         out_shape=outs,
         compiler_params=params(60),
         cost_estimate=cost(1e6, 12e6),
         name="emit",
-    )(place, done, near_in, far_in, sums, late)
+    )(done, near_in, far_in, sums, late)
 
 
 def eight_places(
@@ -1932,7 +1933,6 @@
     )
     orders = jnp.pad(mask_order[:, None, :], ((0, 0), (0, 7), (0, 256 - quarter)))
     reduce_parts = reduce_weight.reshape(8, parts, hidden // (8 * parts), features)
-    place = jnp.stack([lax.axis_index("dp"), place_y]).astype(jnp.int32)
     embedded, input_one, joint, pairs, mixed, probs, mask, targets_here, weights = front(
         mask_count,
         halves(patches),
@@ -1964,7 +1964,7 @@
         embedded,
         mask,
     )
-    outs = emit(parts, place, done, patch_near, patch_far, sums, late)
+    outs = emit(parts, done, patch_near, patch_far, sums, late)
     flat = {0: (), 1: (-1,), 2: (-1,), 4: (-1,), 5: (-1,), 7: (-1,), 8: (-1,), 9: (-1,), 11: (-1,)}
     flat.update({13: (-1,), 15: (-1,), 16: (-1,)})
     return tuple(

time: 215 us -> 215 us (level)
  no operation moved by 1% of the time
where the time goes in v3:
time: 215 us
  Pallas kernels  211 us (98%)
    pallas_call x1, Pallas kernels, back(): pl.pallas_call(partial(back_kernel, counts), grid=(FIRST_NORM + near,), i...  134 us
    pallas_call x1, Pallas kernels, front(): pl.pallas_call(partial(front_kernel, parts), grid=(FRONT_ATTEND + near *...  42.9 us
    pallas_call x1, Pallas kernels, middle(): pl.pallas_call(middle_kernel, grid=(near,), in_specs=[block, block, colum...  27.8 us
    pallas_call x1, Pallas kernels, emit(): pl.pallas_call(partial(emit_kernel, parts), in_specs=[whole] * 5, out_spe...  5.56 us

profile of v3, /device:TPU:0, one launch (start us, length us, event | category | flops | bytes accessed | tf_op | source)
XLA Modules:
  0.0 214.7 jit_solution(5844586773423777304)
XLA Ops:
  0.7 0.7 copy.39
  1.4 0.6 pad.4.clone
  2.0 1.5 stack_lines.1.lines
  3.5 42.9 %front.1 = (bf16[3,288,768]{2,1,0:T(8,128)(2,1)}, bf16[3,288,768]{2,1,0:T(8,128)(2,1)}, bf16[3,6,3,288,128]{4,3,2,1,0:T(8,128)(2,1)}, bf16[3,6,2,288,128]{4,3,2,...) custom-call(s32[6]{0:T(128)} %counts.1, ...), custom_call_target="tpu_custom_call" | custom-call | flops 5000000000 | bytes 40000000 | tf_op jit(solution)/shard_map/front/pallas_call | solution.py:1229
  46.3 27.8 %middle.1 = (bf16[3,6,288,768]{3,2,1,0:T(8,128)(2,1)}, bf16[3,6,288,768]{3,2,1,0:T(8,128)(2,1)}, bf16[3,288,768]{2,1,0:T(8,128)(2,1)}, f32[3,288,1]{2,1,0:T(8,128)}, f32[16,768]{1,0:T(8,128)}) custom-call(bf16[3,288,768]{2,1,0:T(8,128)(2,1)} %get-tuple-element.55.embedded_in, bf16[3,288,768]{2,1,0:T(8,128)(2,1)} %get-tuple-element.56.mixed, ...), custom_call_target="tpu_custom_call" | custom-call | flops 10192158720 | bytes 40000000 | tf_op jit(solution)/shard_map/middle/pallas_call | solution.py:1343
  74.2 133.7 %back.1 = (bf16[13,2,2,48,384]{4,3,2,1,0:T(8,128)(2,1)}, f32[3,144,768]{2,1,0:T(8,128)}, bf16[3,144,768]{2,1,0:T(8,128)(2,1)}, f32[16,768]{1,0:T(8,128)}, f32[8,768]{1,0:T(8,128)}) custom-call(bf16[3,6,288,768]{3,2,1,0:T(8,128)(2,1)} %get-tuple-element.60.left, bf16[3,6,288,768]{3,2,1,0:T(8,128)(2,1)} %get-tuple-element.61.right, ...), custom_call_target="tpu_custom_call" | custom-call | flops 40000000000 | bytes 60000000 | tf_op jit(solution)/shard_map/back/pallas_call | solution.py:1720
  207.9 5.6 %emit.1 = (f32[1]{0:T(128)}, f32[1,96]{1,0:T(1,128)}, f32[1,96]{1,0:T(1,128)}, f32[96,2304]{1,0:T(8,128)}, f32[1,96]{1,0:T(1,128)}, /*index=5*/f32[1,96]{1,0:T(1...) custom-call(bf16[13,2,2,48,384]{4,3,2,1,0:T(8,128)(2,1)} %get-tuple-, ...), custom_call_target="tpu_custom_call" | custom-call | flops 1000000 | bytes 12000000 | tf_op jit(solution)/shard_map/emit/pallas_call | solution.py:1879
  213.4 1.3 reduce
